TPU v7x, 128 devices: a whole 4x4x4 slice. The times are simulated.
128 devices in a mesh: stn: 32 (over y_hi, x, z), tm: 4 (over y_lo, core).
Axes of the slice: x: 4, y: 4 (y_hi: 2, y_lo: 2; y = y_hi * 2 + y_lo), z: 4, core: 2. Of those that a mesh axis runs over, the one named last changes fastest.
Arguments:
- voltages: bfloat16 [2, 512, 262144], P(None, 'stn', 'tm'), may hold values from -6 to 6
- delays: int32 [512], P('stn'), may hold values from 0 to 2048, as said below
- fringe: int32 [512], P('stn'), may hold values from 0 to 4095
- fringe_rate: int32 [512], P('stn'), may hold values from 0 to 4095
- filter_taps: float32 [16, 1024], replicated, may hold values from -1.5 to 1.5
Outputs:
- vis_real: float32 [1024, 512, 512], P(('stn', 'tm'))
- vis_imag: float32 [1024, 512, 512], P(('stn', 'tm'))
Inputs may be any that keep to these rules, and one draw needn't show every extreme that they name: `delays`: the largest delay over all stations is exactly 2048.
All inputs are finite; a program needn't handle non-finite values.
Results may differ from a plain program's by a relative error of at most 0.0066.
Values may be sent and summed in bfloat16 or wider, within the bound.
No kernel may reach another device: no remote copies, remote signals or barrier semaphores. Data moves between devices by JAX's collectives and lax.ppermute only.
A program may use at most 192 MiB of HBM per device.

v0:
```python
import math

import jax
import jax.numpy as jnp
from jax import lax
from jax.sharding import PartitionSpec as P

C = 1024
P_SIZE = 16
Q = 4096
DMAX = 2048


TWO_PI = 2.0 * math.pi


def from_behind(block, axis, distance):
    devices = range(lax.axis_size(axis))
    route = [(i - distance, i) for i in devices if i - distance in devices]
    return lax.ppermute(block, axis, route)


def dft_tables(table_size):
    column = jnp.arange(table_size, dtype=jnp.int32)
    product = column[:, None] * column[None, :] % table_size
    angles = product.astype(jnp.float32) * (TWO_PI / table_size)
    return (jnp.cos(angles).astype(jnp.bfloat16), jnp.sin(angles).astype(jnp.bfloat16))


def channelize(delayed, filter_taps, fringe, fringe_rate, spectra, tables):
    stations = delayed.shape[1]
    blocks = delayed.reshape(2, stations, spectra + P_SIZE - 1, C)
    summed = jnp.zeros((2, stations, spectra, C), jnp.float32)
    for tap_index in range(P_SIZE):
        summed = summed + filter_taps[tap_index] * blocks[
            :, :, tap_index : tap_index + spectra
        ].astype(jnp.float32)
    weighted = summed.astype(jnp.bfloat16)
    weighted_rows = jnp.transpose(weighted, (1, 0, 2, 3)).reshape(stations, 2 * spectra, C)
    cosine_table, sine_table = tables
    with_cosine = jnp.einsum(
        "skn,nc->csk", weighted_rows, cosine_table, preferred_element_type=jnp.float32
    )
    with_sine = jnp.einsum(
        "skn,nc->csk", weighted_rows, sine_table, preferred_element_type=jnp.float32
    )
    inverse_root = 1.0 / math.sqrt(C)
    real_part = (with_cosine[..., :spectra] + with_sine[..., spectra:]) * inverse_root
    imag_part = (with_cosine[..., spectra:] - with_sine[..., :spectra]) * inverse_root
    channel = jnp.arange(C, dtype=jnp.int32)
    phase_index = (fringe[None, :] + fringe_rate[None, :] * channel[:, None]) % Q
    rotation = phase_index.astype(jnp.float32) * (TWO_PI / Q)
    rot_cos = jnp.cos(rotation)[:, :, None]
    rot_sin = jnp.sin(rotation)[:, :, None]
    out_real = real_part * rot_cos - imag_part * rot_sin
    out_imag = real_part * rot_sin + imag_part * rot_cos
    return jnp.concatenate([out_real, out_imag], axis=2).astype(jnp.bfloat16)


def products(left_rows, right_rows, swapped):
    gram_real = jnp.einsum(
        "cak,cbk->cab", left_rows, right_rows, preferred_element_type=jnp.float32
    )
    gram_imag = jnp.einsum("cak,cbk->cab", swapped, right_rows, preferred_element_type=jnp.float32)
    return (gram_real, gram_imag)


def local(voltages, delays, fringe, fringe_rate, filter_taps):
    samples = voltages.shape[2]
    spectra = samples // C
    stations = voltages.shape[1]
    early_rim = from_behind(voltages[:, :, samples - DMAX :], "tm", 1)
    late_rim = from_behind(voltages[:, :, : (P_SIZE - 1) * C], "tm", -1)
    extended = jnp.concatenate([early_rim, voltages, late_rim], axis=2)
    length = samples + (P_SIZE - 1) * C

    def select_window(station_row, delay_value):
        return lax.dynamic_slice_in_dim(station_row, DMAX - delay_value, length, 1)

    delayed = jax.vmap(select_window, in_axes=(1, 0), out_axes=1)(extended, delays)
    turned = channelize(delayed, filter_taps, fringe, fringe_rate, spectra, dft_tables(C))
    outgoing = turned.reshape(C, 1, stations, 2 * spectra)
    stn_count = lax.axis_size("stn")
    tm_count = lax.axis_size("tm")
    whole = stn_count * stations
    received = lax.all_to_all(outgoing, ("stn", "tm"), split_axis=0, concat_axis=1, tiled=True)
    grouped = received.reshape(-1, stn_count, tm_count, stations, 2, spectra)
    ordered = jnp.transpose(grouped, (0, 1, 3, 4, 2, 5))
    width = tm_count * spectra
    rows = ordered.reshape(-1, whole, 2 * width)
    swapped = jnp.concatenate([rows[..., width:], -rows[..., :width]], axis=-1)
    gram_real, gram_imag = products(rows, rows, swapped)
    inverse_count = 1.0 / (spectra * tm_count)
    return (gram_real * inverse_count, gram_imag * inverse_count)


def solution(mesh):
    return jax.shard_map(
        local,
        mesh=mesh,
        in_specs=(P(None, "stn", "tm"), P("stn"), P("stn"), P("stn"), P()),
        out_specs=(P(("stn", "tm"), None, None), P(("stn", "tm"), None, None)),
        check_vma=False,
    )
```

profile of v0, /device:TPU:7, one launch (start us, length us, event | category | flops | bytes accessed | tf_op | source)
XLA Modules:
  0.0 360.6 jit_solution(9335461916052140957)
XLA Ops:
  0.7 6.5 %copy.24 = bf16[2,16,65536]{2,0,1:T(2,128)(2,1)S(1)} copy(bf16[2,16,65536]{2,1,0:T(8,128)(2,1)} %param.5) | data formatting | bytes 8388608 | tf_op args[0]
  15.7 7.8 %collective-permute-done.1 = bf16[2,16,15360]{2,0,1:T(2,128)(2,1)S(1)} collective-permute-done((bf16[2,16,15360]{2,0,1:T(2,128)(2,1)S(1)}, bf16[2,16,15360]{2,0,1:T(2,128)(2,1)S(1)}, u32[]{:S(2)}, u32[]{:S(2)}) %collective-permute-start.1) | collective-permute-done | bytes 983072 | tf_op jit(solution)/shard_map/ppermute | solution.py:20
  23.4 14.5 %maximum_bitcast_fusion = bf16[16,2,82944]{2,1,0:T(2,128)(2,1)} fusion(bf16[2,16,15360]{2,0,1:T(2,128)(2,1)S(1)} %collective-permute-done.1, bf16[2,16,65536]{2,0,1:T(2,128)(2,1)} %copy-done.1, bf16[2,16,2048]{2,0,1:T(2,128)(2,1)S(1)} %collective-permute-done), kind=kLoop, calls=%fused_computation.7 | loop fusion | flops 15925248 | bytes 10616832 | tf_op jit(solution)/shard_map/vmap()/transpose | solution.py:78
  37.9 64.3 %while.1 = (s32[]{:T(128)}, bf16[16,2,82944]{2,1,0:T(2,128)(2,1)}, s32[16,3]{0,1:T(4,128)S(1)}, bf16[16,2,80896]{2,1,0:T(2,128)(2,1)}, s32[]{:T(128)}) while((s32[]{:T(128)}, bf16[16,2,82944]{2,1,0:T(2,128)(2,1)}, s32[16,3]{0,1:T(4,128)S(1)}, bf16[16,2,80896]{2,1,0:T(2,128)(2,1)}, s32[]{:T(128)}) %tuple.56), condition=%wide.while_cond, body=%wide.while_body.sunk | while | flops 2 | bytes 648809 | solution.py:78
  38.6 3.4 dynamic-slice_dynamic-update-slice_fusion.2
  42.6 3.4 dynamic-slice_dynamic-update-slice_fusion.2
  46.6 3.4 dynamic-slice_dynamic-update-slice_fusion.2
  50.6 3.4 dynamic-slice_dynamic-update-slice_fusion.2
  54.6 3.4 dynamic-slice_dynamic-update-slice_fusion.2
  58.7 3.4 dynamic-slice_dynamic-update-slice_fusion.2
  62.7 3.4 dynamic-slice_dynamic-update-slice_fusion.2
  66.7 3.4 dynamic-slice_dynamic-update-slice_fusion.2
  70.7 3.4 dynamic-slice_dynamic-update-slice_fusion.2
  74.7 3.4 dynamic-slice_dynamic-update-slice_fusion.2
  78.7 3.4 dynamic-slice_dynamic-update-slice_fusion.2
  82.8 3.4 dynamic-slice_dynamic-update-slice_fusion.2
  86.8 3.4 dynamic-slice_dynamic-update-slice_fusion.2
  90.8 3.4 dynamic-slice_dynamic-update-slice_fusion.2
  94.8 3.4 dynamic-slice_dynamic-update-slice_fusion.2
  98.8 3.4 dynamic-slice_dynamic-update-slice_fusion.2
  102.2 11.7 %reshape.162 = bf16[2,16,79,1024]{3,2,0,1:T(8,128)(2,1)} reshape(bf16[2,16,80896]{2,0,1:T(2,128)(2,1)} %bitcast.59) | data formatting | bytes 10354688 | tf_op jit(solution)/shard_map/reshape | solution.py:32
  113.9 44.7 %fusion.37 = (bf16[2,16,64,1024]{3,2,0,1:T(8,128)(2,1)S(1)}, bf16[2,16,64,1024]{3,2,0,1:T(8,128)(2,1)S(1)}, bf16[2,16,64,1024]{3,2,0,1:T(8,128)(2,1)S(1)}, bf16[...) fusion(bf16[2,16,79,1024]{3,2,0,1:T(8,128)(2,1)} %reshape.162), kind=kLoop, calls=%fused_computation.56 | loop fusion | bytes 134217728 | tf_op jit(solution)/shard_map/slice | solution.py:35
  158.6 21.4 %fusion.10 = bf16[16,2,64,1024]{3,2,0,1:T(8,128)(2,1)} fusion(bf16[2,16,64,1024]{3,2,0,1:T(8,128)(2,1)} %get-tuple-element.37, f32[1024]{0:T(1024)S(1)} %bitcast.76, bf16[2,16,64,1024]{3,2,0,1:T(8,128)(2,1)S(1)} %get-tuple-element.23, f32[1024]{0:T(1024)S(1)} %bitcast.77, bf16[2,16,64,1024]{3,2,0,1:T(8,128)(2,1)S(1)} %get-tuple-element.24, ...), kind=kLoop, calls=%fused_computation.27 | loop fusion | flops 100663296 | bytes 71368704 | tf_op jit(solution)/shard_map/transpose | solution.py:39
  182.6 21.1 %fusion.14 = f32[1024,16,128]{0,2,1:T(8,128)S(1)} fusion(bf16[16,128,1024]{2,1,0:T(8,128)(2,1)S(1)} %bitcast.60), kind=kOutput, calls=%fused_computation.29 | convolution fusion | flops 4310695936 | bytes 12582912 | tf_op jit(solution)/shard_map/skn,nc->csk/dot_general | solution.py:41
  203.7 21.5 %fusion.17 = f32[1024,16,128]{0,2,1:T(8,128)S(1)} fusion(bf16[16,128,1024]{2,1,0:T(8,128)(2,1)S(1)} %bitcast.61), kind=kOutput, calls=%fused_computation.31 | convolution fusion | flops 4310695936 | bytes 12582912 | tf_op jit(solution)/shard_map/skn,nc->csk/dot_general | solution.py:44
  230.2 6.8 %copy.29 = bf16[1024,1,16,128]{3,2,1,0:T(8,128)(2,1)} copy(bf16[1024,1,16,128]{0,3,2,1:T(8,128)(2,1)} %pad_maximum_fusion) | data formatting | bytes 8388608 | tf_op jit(solution)/shard_map/concatenate | solution.py:57
  237.0 65.3 %all_to_all.15 = bf16[1024,1,16,128]{3,2,1,0:T(8,128)(2,1)} all-to-all(bf16[1024,1,16,128]{3,2,1,0:T(8,128)(2,1)} %copy.29), channel_id=1, replica_groups=mesh['stn'=32,'tm'=4] {'stn','tm'}, dimensions={0} | all-to-all | bytes 8388608 | tf_op jit(solution)/shard_map/all_to_all | solution.py:86
  302.3 14.7 %reshape.135 = bf16[8,32,4,16,2,64]{5,4,3,0,2,1:T(2,128)(2,1)} reshape(bf16[8,128,1,16,128]{4,3,0,1,2:T(8,128)(2,1)} %bitcast.58) | data formatting | bytes 8388608 | tf_op jit(solution)/shard_map/reshape | solution.py:87
  317.0 14.7 %copy.97 = bf16[8,32,4,16,2,64]{5,2,4,3,1,0:T(4,128)(2,1)} copy(bf16[8,32,4,16,2,64]{5,4,3,0,2,1:T(2,128)(2,1)} %reshape.135) | data formatting | bytes 8388608 | tf_op jit(solution)/shard_map/reshape | solution.py:87
  331.7 13.9 %reshape.136 = bf16[8,512,512]{2,1,0:T(8,128)(2,1)} reshape(bf16[8,32,16,2,4,64]{5,4,3,2,1,0:T(4,128)(2,1)} %bitcast.57) | data formatting | bytes 8388608 | tf_op jit(solution)/shard_map/reshape | solution.py:90
  349.0 5.8 %broadcast_multiply_fusion.1 = f32[8,512,512]{2,1,0:T(8,128)} fusion(bf16[8,512,512]{2,1,0:T(8,128)(2,1)S(1)} %copy-done), kind=kOutput, calls=%fused_computation.19 | convolution fusion | flops 2149580800 | bytes 12582912 | tf_op jit(solution)/shard_map/cak,cbk->cab/dot_general | solution.py:61
  354.8 5.8 %broadcast_multiply_fusion = f32[8,512,512]{2,1,0:T(8,128)} fusion(bf16[8,512,512]{2,1,0:T(8,128)(2,1)S(1)} %copy-done, bf16[8,512,256]{2,1,0:T(8,128)(2,1)S(1)} %get-tuple-element.39, bf16[8,512,256]{2,1,0:T(8,128)(2,1)S(1)} %get-tuple-element.38), kind=kOutput, calls=%fused_computation.18 | convolution fusion | flops 2157969408 | bytes 16777216 | tf_op jit(solution)/shard_map/cak,cbk->cab/dot_general | solution.py:64
  (59 shorter events, 29.8 us)
Async XLA Ops:
  0.6 13.1 %copy-start.2 = (f32[16,1024]{1,0:T(8,128)S(1)}, f32[16,1024]{1,0:T(8,128)}, u32[]{:S(2)}) copy-start(f32[16,1024]{1,0:T(8,128)} %param.9) | copy-start | bytes 196612
  0.6 13.2 %copy-start.4 = (s32[16]{0:T(128)S(1)}, s32[16]{0:T(128)}, u32[]{:S(2)}) copy-start(s32[16]{0:T(128)} %param.7) | copy-start | bytes 196
  0.7 13.2 %copy-start.3 = (s32[16]{0:T(128)S(1)}, s32[16]{0:T(128)}, u32[]{:S(2)}) copy-start(s32[16]{0:T(128)} %param.8) | copy-start | bytes 196
  0.7 13.5 %copy-start.5 = (s32[16]{0:T(128)S(1)}, s32[16]{0:T(128)}, u32[]{:S(2)}) copy-start(s32[16]{0:T(128)} %param.6) | copy-start | bytes 196
  7.2 3.3 copy-start.1
  7.9 15.5 %collective-permute-start.1 = (bf16[2,16,15360]{2,0,1:T(2,128)(2,1)S(1)}, bf16[2,16,15360]{2,0,1:T(2,128)(2,1)S(1)}, u32[]{:S(2)}, u32[]{:S(2)}) collective-permute-start(bf16[2,16,15360]{2,0,1:T(2,128)(2,1)S(1)} %slice.175), channel_id=1, source_target_pairs={{1,0},{2,1},{3,2},{5,4},{6,5},{7,6},{9,8},{10,9},{11,10},{13,12},{... | collective-permute-start | bytes 2949128 | tf_op jit(solution)/shard_map/ppermute | solution.py:20
  10.6 5.0 %collective-permute-start = (bf16[2,16,2048]{2,0,1:T(2,128)(2,1)S(1)}, bf16[2,16,2048]{2,0,1:T(2,128)(2,1)S(1)}, u32[]{:S(2)}, u32[]{:S(2)}) collective-permute-start(bf16[2,16,2048]{2,0,1:T(2,128)(2,1)S(1)} %slice.174), channel_id=1, source_target_pairs={{0,1},{1,2},{2,3},{4,5},{5,6},{6,7},{8,9},{9,10},{10,11},{12,13},{... | collective-permute-start | bytes 393224 | tf_op jit(solution)/shard_map/ppermute | solution.py:20
  345.6 3.4 copy-start
where the time goes:
time: 363 us; the launch traced here: 361 us
  local copies, waits for them, and re-layouts  181 us (50%)
  blocking collectives  65.3 us (18%)
  matrix products  54.1 us (15%)
  other arithmetic  43.9 us (12%)
  waiting for transfers between devices  9.23 us (3%)
  starting transfers between devices  5.69 us (2%)
    all_to_all x1, blocking collectives, local(): lax.all_to_all(outgoing, ('stn', 'tm'), split_axis=0, concat_axis=1, tile...  65.3 us
    gather x48, local copies, waits for them, and re-layouts  64.2 us
    slice x1, local copies, waits for them, and re-layouts, channelize(): blocks[:, :, tap_index:tap_index + spectra].astype(jnp.float32)  44.7 us
    reshape x2, local copies, waits for them, and re-layouts, local(): grouped = received.reshape(-1, stn_count, tm_count, stations, 2, spectra)  29.3 us
    dot_general x1, matrix products, channelize(): jnp.einsum('skn,nc->csk', weighted_rows, sine_table, preferred_element_ty...  21.5 us
    transpose x1, other arithmetic, channelize(): jnp.transpose(weighted, (1, 0, 2, 3)).reshape(stations, 2 * spectra, C)  21.4 us
    dot_general x1, matrix products, channelize(): jnp.einsum('skn,nc->csk', weighted_rows, cosine_table, preferred_element_...  21.1 us
    transpose x1, other arithmetic, select_window(): return lax.dynamic_slice_in_dim(station_row, DMAX - delay_value, length, 1)  14.5 us
  transfers between devices with their start and end apart: 2, of which 2 were waited for; matrix products, arithmetic and copies ran while one was open for 0% of the time, Pallas kernels for 0%

commit v1 on v0

v1 whole, which is shorter than its diff:
```python
import math

import jax
import jax.numpy as jnp
import numpy as np
from jax import lax
from jax.experimental import pallas as pl
from jax.experimental.pallas import tpu as pltpu
from jax.sharding import PartitionSpec as P

C = 1024
P_SIZE = 16
Q = 4096
DMAX = 2048
LANES = 128
SUB = 8
RADIX = 4
K = C // RADIX
TWO_PI = 2.0 * math.pi
BF16 = jnp.bfloat16
F32 = jnp.float32


def from_behind(block, axis, distance):
    devices = range(lax.axis_size(axis))
    route = [(i - distance, i) for i in devices if i - distance in devices]
    return lax.ppermute(block, axis, route)


def dft_table():
    channel = (RADIX * np.arange(K)[None, :] + np.arange(RADIX)[:, None]).reshape(C)
    angle = (channel[:, None] * np.arange(K)[None, :] % C) * (TWO_PI / C)
    return np.concatenate([np.cos(angle), np.sin(angle)], axis=1).astype(BF16)


def rotation_tables(fringe, fringe_rate):
    channel = (RADIX * jnp.arange(K)[None, :] + jnp.arange(RADIX)[:, None]).reshape(C)
    phase = (fringe[None, :] + fringe_rate[None, :] * channel[:, None]) % Q
    angle = phase.astype(F32) * (TWO_PI / Q)
    scale = 1.0 / math.sqrt(C)
    return jnp.cos(angle) * scale, jnp.sin(angle) * scale


EARLY = DMAX // LANES
LATE = (P_SIZE - 1) * C // LANES
ROW_PAD = 8


def front_kernel(
    delays, volts, early, late, taps, table, rot_cos, rot_sin, out, lin, filt, zs, turned
):
    stations, samples = volts.shape[1], volts.shape[2]
    frames = samples // C
    blocks = samples // LANES
    row_step = lin.shape[0] // (2 * stations)

    def spread(source, count, offset, unroll):
        def body(step, carry):
            for inner in range(unroll):
                block = step * unroll + inner
                lanes = pl.ds(pl.multiple_of(block * LANES, LANES), LANES)
                for part in range(2):
                    tile = source[part, :, lanes].astype(F32)
                    for top in range(0, stations, SUB):
                        start = (part * stations + top) * row_step + ROW_PAD + offset + block
                        lin[pl.ds(start, SUB, stride=row_step), :] = tile[top : top + SUB]
            return carry

        lax.fori_loop(0, count // unroll, body, 0)

    spread(early, EARLY, 0, 8)
    spread(volts, blocks, EARLY, 8)
    spread(late, LATE, EARLY + blocks, 8)

    lane = lax.broadcasted_iota(jnp.int32, (SUB, LANES), 1)

    def filter_row(row, carry):
        delay = delays[row % stations]
        shift = delay % LANES
        base = row * row_step + ROW_PAD + EARLY - delay // LANES
        keep = lane < LANES - shift
        sums = {}
        for k in range(frames + P_SIZE - 1):
            here = lin[pl.ds(base + SUB * k, SUB), :]
            before = lin[pl.ds(base + SUB * k - 1, SUB), :]
            frame = pltpu.roll(jnp.where(keep, here, before), shift, 1)
            for p in range(P_SIZE):
                m = k - p
                if 0 <= m < frames:
                    term = taps[SUB * p : SUB * (p + 1), :] * frame
                    sums[m] = sums[m] + term if m in sums else term
            m = k - (P_SIZE - 1)
            if m >= 0:
                start = pl.multiple_of(row * (frames * SUB), SUB) + m * SUB
                filt[pl.ds(start, SUB), :] = sums.pop(m)
        return carry

    lax.fori_loop(0, 2 * stations, filter_row, 0)

    def butterflies(s, carry):
        def load(part, j):
            start = (part * stations + s) * (frames * SUB) + j
            return filt[pl.ds(start, frames, stride=SUB), :]

        for half in range(2):
            re = [load(0, 2 * q + half) for q in range(4)]
            im = [load(1, 2 * q + half) for q in range(4)]
            re_e, re_d = re[0] + re[2], re[0] - re[2]
            im_e, im_d = im[0] + im[2], im[0] - im[2]
            re_f, re_g = re[1] + re[3], re[1] - re[3]
            im_f, im_g = im[1] + im[3], im[1] - im[3]
            z = [
                (re_e + re_f, im_e + im_f),
                (re_d + im_g, im_d - re_g),
                (re_e - re_f, im_e - im_f),
                (re_d - im_g, im_d + re_g),
            ]
            for r in range(RADIX):
                zr, zi = z[r][0].astype(BF16), z[r][1].astype(BF16)
                top = pl.multiple_of(s * 2 * frames, 2 * frames)
                cols = pl.ds(half * LANES, LANES)
                cols_sin = pl.ds(K + half * LANES, LANES)
                zs[r, pl.ds(top, frames), cols] = zr
                zs[r, pl.ds(top, frames), cols_sin] = zi
                zs[r, pl.ds(top + frames, frames), cols] = zi
                zs[r, pl.ds(top + frames, frames), cols_sin] = -zr
        return carry

    lax.fori_loop(0, stations, butterflies, 0)

    width = 2 * frames
    sign = jnp.where(lax.broadcasted_iota(jnp.int32, (1, width), 1) < frames, -1.0, 1.0)

    def transform(r, carry):
        rows = pl.ds(pl.multiple_of(r * K, K), K)
        weights = table[rows, :]
        cosines = rot_cos[rows, :]
        sines = rot_sin[rows, :]
        for s0 in range(0, stations, 2):
            both = lax.dot_general(
                weights,
                zs[r, s0 * width : (s0 + 2) * width, :],
                (((1,), (1,)), ((), ())),
                preferred_element_type=F32,
            )
            for s in (s0, s0 + 1):
                spec = both[:, (s - s0) * width : (s - s0 + 1) * width]
                cross = pltpu.roll(spec, frames, 1) * sign
                rotated = spec * cosines[:, s : s + 1] + cross * sines[:, s : s + 1]
                turned[pl.ds(s, K, stride=stations), :] = rotated
        for k0 in range(0, K, 16):
            piece = turned[k0 * stations : (k0 + 16) * stations, :].astype(BF16)
            out[k0 : k0 + 16, r] = piece.reshape(16, stations, width)
        return carry

    lax.fori_loop(0, RADIX, transform, 0)


def front(delays, voltages, early, late, filter_taps, fringe, fringe_rate):
    stations, samples = voltages.shape[1], voltages.shape[2]
    frames = samples // C
    blocks = samples // LANES
    row_step = ROW_PAD + EARLY + blocks + LATE + 1
    rot_cos, rot_sin = rotation_tables(fringe, fringe_rate)
    taps = filter_taps.reshape(P_SIZE * SUB, LANES)
    vmem = pl.BlockSpec(memory_space=pltpu.VMEM)
    smem = pl.BlockSpec(memory_space=pltpu.SMEM)
    return pl.pallas_call(
        front_kernel,
        out_shape=jax.ShapeDtypeStruct((K, RADIX, stations, 2 * frames), BF16),
        in_specs=[smem] + [vmem] * 7,
        out_specs=vmem,
        scratch_shapes=[
            pltpu.VMEM((-(-(2 * stations * row_step) // 8) * 8, LANES), F32),
            pltpu.VMEM((2 * stations * frames * SUB, LANES), F32),
            pltpu.VMEM((RADIX, stations * 2 * frames, 2 * K), BF16),
            pltpu.VMEM((K * stations, LANES), F32),
        ],
        compiler_params=pltpu.CompilerParams(vmem_limit_bytes=56 * 1024 * 1024),
        name="front",
    )(delays, voltages, early, late, taps, jnp.asarray(dft_table()), rot_cos, rot_sin)


def gram_kernel(scale, groups, times, received, real, imag):
    stations, width = received.shape[1], received.shape[2]
    half = width // 2
    tiles = received[...].reshape(groups, times, stations, width)
    direct, swapped = [], []
    for t in range(times):
        tile = tiles[:, t].reshape(groups * stations, width)
        direct.append(tile)
        swapped.append(jnp.concatenate([tile[:, half:], -tile[:, :half]], axis=1))
    rows = jnp.concatenate(direct, axis=1)
    turned_rows = jnp.concatenate(swapped, axis=1)
    contract = (((1,), (1,)), ((), ()))
    real[0] = lax.dot_general(rows, rows, contract, preferred_element_type=F32) * scale
    imag[0] = lax.dot_general(turned_rows, rows, contract, preferred_element_type=F32) * scale


def gram(received, groups, times):
    devices, channels, stations, width = received.shape
    whole = groups * stations
    scale = 1.0 / (times * width // 2)
    shape = jax.ShapeDtypeStruct((channels, whole, whole), F32)
    block = pl.BlockSpec((1, whole, whole), lambda c: (c, 0, 0))

    def body(received, real, imag):
        gram_kernel(scale, groups, times, received, real, imag)

    return pl.pallas_call(
        body,
        grid=(channels,),
        out_shape=(shape, shape),
        in_specs=[pl.BlockSpec((devices, None, stations, width), lambda c: (0, c, 0, 0))],
        out_specs=(block, block),
        compiler_params=pltpu.CompilerParams(vmem_limit_bytes=48 * 1024 * 1024),
        name="gram",
    )(received)


def local(voltages, delays, fringe, fringe_rate, filter_taps):
    samples = voltages.shape[2]
    stations = voltages.shape[1]
    frames = samples // C
    early = from_behind(voltages[:, :, samples - DMAX :], "tm", 1)
    late = from_behind(voltages[:, :, : (P_SIZE - 1) * C], "tm", -1)
    turned = front(delays, voltages, early, late, filter_taps, fringe, fringe_rate)
    groups, times = lax.axis_size("stn"), lax.axis_size("tm")
    devices = groups * times
    outgoing = turned.reshape(devices, C // devices, stations, 2 * frames)
    received = lax.all_to_all(outgoing, ("stn", "tm"), split_axis=0, concat_axis=0, tiled=True)
    return gram(received, groups, times)


def solution(mesh):
    return jax.shard_map(
        local,
        mesh=mesh,
        in_specs=(P(None, "stn", "tm"), P("stn"), P("stn"), P("stn"), P()),
        out_specs=(P(("stn", "tm"), None, None), P(("stn", "tm"), None, None)),
        check_vma=False,
    )
```

time: 363 us -> 123 us (0.34)
  local copies, waits for them, and re-layouts: 181 us -> 4.01 us
  matrix products: 54.1 us -> 0 us
  other arithmetic: 43.9 us -> 3.58 us
  Pallas kernels: 0 us -> 39.1 us
  waiting for transfers between devices: 9.23 us -> 4.46 us
    gather x48 -> x0, local copies, waits for them, and re-layouts: 64.2 us -> none
    reshape x4 -> x1, local copies, waits for them, and re-layouts: 55 us -> 0.65 us  [front(): taps = filter_taps.reshape(P_SIZE * SUB, LANES)]
    dot_general x4 -> x0, matrix products: 54.1 us -> none  [the longest x1 21.5 us: channelize(): jnp.einsum('skn,nc->csk', weighted_rows, sine_table, preferred_element_ty...]
    slice x4 -> x2, local copies, waits for them, and re-layouts: 45.5 us -> 2.22 us  [the longest x1 1.3 us: local(): late = from_behind(voltages[:, :, :(P_SIZE - 1) * C], 'tm', -1)]
    pallas_call x0 -> x2, Pallas kernels: none -> 39.1 us  [the longest x1 30.9 us: front(): pl.pallas_call(front_kernel, out_shape=jax.ShapeDtypeStruct((K, RADIX, st...]
    transpose x2 -> x0, other arithmetic: 35.9 us -> none  [the longest x1 21.4 us: channelize(): jnp.transpose(weighted, (1, 0, 2, 3)).reshape(stations, 2 * spectra, C)]
    concatenate x1 -> x0, local copies, waits for them, and re-layouts: 6.8 us -> none  [channelize(): return jnp.concatenate([out_real, out_imag], axis=2).astype(jnp.bfloat16)]
    unnamed x14 -> x7, local copies, waits for them, and re-layouts: 7.37 us -> 0.95 us
  transfers between devices with their start and end apart: 2 -> 2, of which waited for: 2 -> 1; matrix products, arithmetic and copies ran while one was open for 0% -> 4% of each run, Pallas kernels for 0% -> 0%
where the time goes in v1:
time: 123 us; the launch traced here: 122 us
  blocking collectives  64.6 us (53%)
  Pallas kernels  39.1 us (32%)
  starting transfers between devices  5.69 us (5%)
  waiting for transfers between devices  4.46 us (4%)
  local copies, waits for them, and re-layouts  4.01 us (3%)
  other arithmetic  3.58 us (3%)
    all_to_all x1, blocking collectives, local(): lax.all_to_all(outgoing, ('stn', 'tm'), split_axis=0, concat_axis=0, tile...  64.6 us
    pallas_call x1, Pallas kernels, front(): pl.pallas_call(front_kernel, out_shape=jax.ShapeDtypeStruct((K, RADIX, st...  30.9 us
    pallas_call x1, Pallas kernels, gram(): pl.pallas_call(body, grid=(channels,), out_shape=(shape, shape), in_specs...  8.25 us
    ppermute x2, starting transfers between devices, from_behind(): return lax.ppermute(block, axis, route)  5.69 us
    ppermute x2, waiting for transfers between devices, from_behind(): return lax.ppermute(block, axis, route)  4.46 us
    mul x1, other arithmetic, rotation_tables(): return (jnp.cos(angle) * scale, jnp.sin(angle) * scale)  2.79 us
  transfers between devices with their start and end apart: 2, of which 1 were waited for; matrix products, arithmetic and copies ran while one was open for 4% of the time, Pallas kernels for 0%

profile of v1, /device:TPU:7, one launch (start us, length us, event | category | flops | bytes accessed | tf_op | source)
XLA Modules:
  0.0 122.1 jit_solution(13943536540546849699)
XLA Ops:
  0.6 0.0 copy-start.2
  0.6 1.3 %slice.7 = bf16[2,16,15360]{2,1,0:T(8,128)(2,1)S(1)} slice(bf16[2,16,65536]{2,1,0:T(8,128)(2,1)} %volts.1), slice={[0:2], [0:16], [0:15360]} | slice | bytes 1966080 | tf_op jit(solution)/shard_map/slice | solution.py:226
  1.9 2.6 %collective-permute-start.1 = (bf16[2,16,15360]{2,1,0:T(8,128)(2,1)S(1)}, bf16[2,16,15360]{2,1,0:T(8,128)(2,1)S(1)}, u32[]{:S(2)}, u32[]{:S(2)}) collective-permute-start(bf16[2,16,15360]{2,1,0:T(8,128)(2,1)S(1)} %slice.7), channel_id=1, source_target_pairs={{1,0},{2,1},{3,2},{5,4},{6,5},{7,6},{9,8},{10,9},{11,10},{13,12},{... | collective-permute-start | bytes 2949128 | tf_op jit(solution)/shard_map/ppermute | solution.py:27
  4.5 0.9 slice.6
  5.5 3.1 %collective-permute-start = (bf16[2,16,2048]{2,1,0:T(8,128)(2,1)S(1)}, bf16[2,16,2048]{2,1,0:T(8,128)(2,1)S(1)}, u32[]{:S(2)}, u32[]{:S(2)}) collective-permute-start(bf16[2,16,2048]{2,1,0:T(8,128)(2,1)S(1)} %slice.6), channel_id=1, source_target_pairs={{0,1},{1,2},{2,3},{4,5},{5,6},{6,7},{8,9},{9,10},{10,11},{12,13},{... | collective-permute-start | bytes 393224 | tf_op jit(solution)/shard_map/ppermute | solution.py:27
  8.6 0.8 fusion.1
  9.4 0.2 copy.8
  9.6 2.8 %sine_multiply_fusion = (f32[1024,16]{1,0:T(8,128)}, f32[1024,16]{1,0:T(8,128)}) fusion(f32[1024,16]{1,0:T(8,128)S(1)} %copy.8), kind=kLoop, calls=%fused_computation | loop fusion | flops 49152 | bytes 196608 | tf_op jit(solution)/shard_map/mul | solution.py:41
  12.4 0.0 copy-done.2
  12.4 0.6 reshape.31.taps
  13.0 0.0 collective-permute-done.early
  13.0 0.0 copy-start.1
  13.0 4.5 %collective-permute-done.1.late = bf16[2,16,15360]{2,1,0:T(8,128)(2,1)S(1)} collective-permute-done((bf16[2,16,15360]{2,1,0:T(8,128)(2,1)S(1)}, bf16[2,16,15360]{2,1,0:T(8,128)(2,1)S(1)}, u32[]{:S(2)}, u32[]{:S(2)}) %collective-permute-start.1) | collective-permute-done | bytes 983072 | tf_op jit(solution)/shard_map/ppermute | solution.py:27
  17.5 0.0 copy-start
  17.5 0.0 copy-done.1
  17.5 0.9 copy-done
  18.4 30.9 %front.1 = bf16[256,4,16,128]{3,2,1,0:T(8,128)(2,1)} custom-call(s32[16]{0:T(128)} %delays.1, bf16[2,16,65536]{2,1,0:T(8,128)(2,1)} %volts.1, bf16[2,16,2048]{2,1,0:T(8,128)(2,1)} %copy-done.1, bf16[2,16,15360]{2,1,0:T(8,128)(2,1)} %copy-done, f32[128,128]{1,0:T(8,128)} %reshape.31.taps, bf16[1024,512]{1,0:T(8,128)(2,1)} %constant.23.clone.table, ...), custom_call_target="tpu_custom_call" | custom-call | tf_op jit(solution)/shard_map/front/pallas_call | solution.py:168
  49.3 64.6 %all_to_all.5.received = bf16[128,8,16,128]{3,2,1,0:T(8,128)(2,1)S(1)} all-to-all(bf16[128,8,16,128]{3,2,1,0:T(8,128)(2,1)} %bitcast.4), channel_id=1, replica_groups=mesh['stn'=32,'tm'=4] {'stn','tm'}, dimensions={0} | all-to-all | bytes 8388608 | tf_op jit(solution)/shard_map/all_to_all | solution.py:231
  113.9 8.2 %gram.1 = (f32[8,512,512]{2,1,0:T(8,128)}, f32[8,512,512]{2,1,0:T(8,128)}) custom-call(bf16[128,8,16,128]{3,2,1,0:T(8,128)(2,1)S(1)} %all_to_all.5.received), custom_call_target="tpu_custom_call" | custom-call | tf_op jit(solution)/shard_map/gram/pallas_call | solution.py:210
  (3 shorter events, 0.0 us)
Async XLA Ops:
  0.6 11.7 %copy-start.2 = (f32[16,1024]{1,0:T(8,128)S(1)}, f32[16,1024]{1,0:T(8,128)}, u32[]{:S(2)}) copy-start(f32[16,1024]{1,0:T(8,128)} %param.10) | copy-start | bytes 196612
  1.9 15.5 %collective-permute-start.1 = (bf16[2,16,15360]{2,1,0:T(8,128)(2,1)S(1)}, bf16[2,16,15360]{2,1,0:T(8,128)(2,1)S(1)}, u32[]{:S(2)}, u32[]{:S(2)}) collective-permute-start(bf16[2,16,15360]{2,1,0:T(8,128)(2,1)S(1)} %slice.7), channel_id=1, source_target_pairs={{1,0},{2,1},{3,2},{5,4},{6,5},{7,6},{9,8},{10,9},{11,10},{13,12},{... | collective-permute-start | bytes 2949128 | tf_op jit(solution)/shard_map/ppermute | solution.py:27
  5.5 7.6 %collective-permute-start = (bf16[2,16,2048]{2,1,0:T(8,128)(2,1)S(1)}, bf16[2,16,2048]{2,1,0:T(8,128)(2,1)S(1)}, u32[]{:S(2)}, u32[]{:S(2)}) collective-permute-start(bf16[2,16,2048]{2,1,0:T(8,128)(2,1)S(1)} %slice.6), channel_id=1, source_target_pairs={{0,1},{1,2},{2,3},{4,5},{5,6},{6,7},{8,9},{9,10},{10,11},{12,13},{... | collective-permute-start | bytes 393224 | tf_op jit(solution)/shard_map/ppermute | solution.py:27
  13.0 4.5 %copy-start.1 = (bf16[2,16,2048]{2,1,0:T(8,128)(2,1)}, bf16[2,16,2048]{2,1,0:T(8,128)(2,1)S(1)}, u32[]{:S(2)}) copy-start(bf16[2,16,2048]{2,1,0:T(8,128)(2,1)S(1)} %collective-permute-done.early) | copy-start | bytes 393220
  17.5 0.9 copy-start

commit v2 on v1

--- a/solution.py
+++ b/solution.py
@@ -34,44 +34,40 @@
 
 
 def rotation_tables(fringe, fringe_rate):
-    channel = (RADIX * jnp.arange(K)[None, :] + jnp.arange(RADIX)[:, None]).reshape(C)
-    phase = (fringe[None, :] + fringe_rate[None, :] * channel[:, None]) % Q
-    angle = phase.astype(F32) * (TWO_PI / Q)
+    fine = (fringe[:, None] + fringe_rate[:, None] * jnp.arange(RADIX)[None, :]) % Q
+    fine = fine.astype(F32) * (TWO_PI / Q)
     scale = 1.0 / math.sqrt(C)
-    return jnp.cos(angle) * scale, jnp.sin(angle) * scale
+    phases = jnp.stack([jnp.cos(fine) * scale, jnp.sin(fine) * scale], axis=2).reshape(-1)
+    coarse = (RADIX * fringe_rate[:, None] * jnp.arange(K)[None, :]) % Q
+    coarse = coarse.astype(F32) * (TWO_PI / Q)
+    coarse = lax.optimization_barrier(jnp.concatenate([jnp.cos(coarse), jnp.sin(coarse)]))
+    return phases, coarse.T
 
 
 EARLY = DMAX // LANES
 LATE = (P_SIZE - 1) * C // LANES
 ROW_PAD = 8
-
-
-def front_kernel(
-    delays, volts, early, late, taps, table, rot_cos, rot_sin, out, lin, filt, zs, turned
-):
-    stations, samples = volts.shape[1], volts.shape[2]
-    frames = samples // C
-    blocks = samples // LANES
-    row_step = lin.shape[0] // (2 * stations)
-
-    def spread(source, count, offset, unroll):
-        def body(step, carry):
-            for inner in range(unroll):
-                block = step * unroll + inner
-                lanes = pl.ds(pl.multiple_of(block * LANES, LANES), LANES)
-                for part in range(2):
-                    tile = source[part, :, lanes].astype(F32)
-                    for top in range(0, stations, SUB):
-                        start = (part * stations + top) * row_step + ROW_PAD + offset + block
-                        lin[pl.ds(start, SUB, stride=row_step), :] = tile[top : top + SUB]
-            return carry
-
-        lax.fori_loop(0, count // unroll, body, 0)
-
-    spread(early, EARLY, 0, 8)
-    spread(volts, blocks, EARLY, 8)
-    spread(late, LATE, EARLY + blocks, 8)
-
+STEP = SUB + 1
+
+
+def spread(source, first, count, offset, stations, row_step, lin):
+    unroll = 8
+
+    def body(step, carry):
+        for inner in range(unroll):
+            block = step * unroll + inner
+            lanes = pl.ds(pl.multiple_of((first + block) * LANES, LANES), LANES)
+            for part in range(2):
+                tile = source[part, :, lanes].astype(F32)
+                for top in range(0, stations, SUB):
+                    start = (part * stations + top) * row_step + ROW_PAD + offset + block
+                    lin[pl.ds(start, SUB, stride=row_step), :] = tile[top : top + SUB]
+        return carry
+
+    lax.fori_loop(0, count // unroll, body, 0)
+
+
+def filter_frames(delays, taps, stations, frames, row_step, lin, filt):
     lane = lax.broadcasted_iota(jnp.int32, (SUB, LANES), 1)
 
     def filter_row(row, carry):
@@ -91,16 +87,17 @@
                     sums[m] = sums[m] + term if m in sums else term
             m = k - (P_SIZE - 1)
             if m >= 0:
-                start = pl.multiple_of(row * (frames * SUB), SUB) + m * SUB
-                filt[pl.ds(start, SUB), :] = sums.pop(m)
+                filt[pl.ds((row * frames + m) * STEP, SUB), :] = sums.pop(m)
         return carry
 
-    lax.fori_loop(0, 2 * stations, filter_row, 0)
-
-    def butterflies(s, carry):
+    lax.fori_loop(0, 2 * stations, filter_row, 0, unroll=2)
+
+
+def butterflies(phases, stations, frames, filt, zs):
+    def body(s, carry):
         def load(part, j):
-            start = (part * stations + s) * (frames * SUB) + j
-            return filt[pl.ds(start, frames, stride=SUB), :]
+            start = (part * stations + s) * (frames * STEP) + j
+            return filt[pl.ds(start, frames, stride=STEP), :]
 
         for half in range(2):
             re = [load(0, 2 * q + half) for q in range(4)]
@@ -116,69 +113,132 @@
                 (re_d - im_g, im_d + re_g),
             ]
             for r in range(RADIX):
-                zr, zi = z[r][0].astype(BF16), z[r][1].astype(BF16)
-                top = pl.multiple_of(s * 2 * frames, 2 * frames)
-                cols = pl.ds(half * LANES, LANES)
-                cols_sin = pl.ds(K + half * LANES, LANES)
-                zs[r, pl.ds(top, frames), cols] = zr
-                zs[r, pl.ds(top, frames), cols_sin] = zi
-                zs[r, pl.ds(top + frames, frames), cols] = zi
-                zs[r, pl.ds(top + frames, frames), cols_sin] = -zr
+                cosine = phases[(s * RADIX + r) * 2]
+                sine = phases[(s * RADIX + r) * 2 + 1]
+                zr = z[r][0] * cosine - z[r][1] * sine
+                zi = z[r][0] * sine + z[r][1] * cosine
+                zs[r, s, :, pl.ds(half * LANES, LANES)] = zr.astype(BF16)
+                zs[r, s, :, pl.ds(K + half * LANES, LANES)] = zi.astype(BF16)
         return carry
 
-    lax.fori_loop(0, stations, butterflies, 0)
-
-    width = 2 * frames
-    sign = jnp.where(lax.broadcasted_iota(jnp.int32, (1, width), 1) < frames, -1.0, 1.0)
-
-    def transform(r, carry):
-        rows = pl.ds(pl.multiple_of(r * K, K), K)
-        weights = table[rows, :]
-        cosines = rot_cos[rows, :]
-        sines = rot_sin[rows, :]
+    lax.fori_loop(0, stations, body, 0)
+
+
+def first_kernel(delays, phases, volts, early, taps, zs, lin, filt):
+    stations, samples = volts.shape[1], volts.shape[2]
+    frames = zs.shape[2]
+    row_step = lin.shape[0] // (2 * stations)
+    spread(early, 0, EARLY, 0, stations, row_step, lin)
+    spread(volts, 0, samples // LANES, EARLY, stations, row_step, lin)
+    filter_frames(delays, taps, stations, frames, row_step, lin, filt)
+    butterflies(phases, stations, frames, filt, zs)
+
+
+def second_kernel(
+    delays, phases, volts, late, taps, table, coarse, before, out,
+    lin, filt, zs, cosines, sines, turned, packed, sems
+):
+    stations = volts.shape[1]
+    done, frames = before.shape[2], zs.shape[2]
+    width = 2 * (done + frames)
+    row_step = lin.shape[0] // (2 * stations)
+    sign = jnp.where(lax.broadcasted_iota(jnp.int32, (1, width), 1) < width // 2, -1.0, 1.0)
+    for s in range(stations):
+        rows = slice(s * K, (s + 1) * K)
+        cosines[rows, :] = jnp.broadcast_to(coarse[:, s : s + 1], (K, width))
+        sines[rows, :] = coarse[:, stations + s : stations + s + 1] * sign
+    blocks = frames * C // LANES + EARLY
+    spread(volts, volts.shape[2] // LANES - blocks, blocks, 0, stations, row_step, lin)
+    spread(late, 0, LATE, blocks, stations, row_step, lin)
+    filter_frames(delays, taps, stations, frames, row_step, lin, filt)
+    butterflies(phases, stations, frames, filt, zs)
+
+    def sent(r, slot):
+        return pltpu.make_async_copy(packed.at[slot], out.at[:, r], sems.at[slot])
+
+    for r in range(RADIX):
+        slot = r % 2
+        weights = table[r * K : (r + 1) * K, :]
         for s0 in range(0, stations, 2):
+            sides = []
+            for s in (s0, s0 + 1):
+                z = jnp.concatenate([before[r, s], zs[r, s]], axis=0)
+                sides += [z, jnp.concatenate([z[:, K:], -z[:, :K]], axis=1)]
             both = lax.dot_general(
                 weights,
-                zs[r, s0 * width : (s0 + 2) * width, :],
+                jnp.concatenate(sides, axis=0),
                 (((1,), (1,)), ((), ())),
                 preferred_element_type=F32,
             )
             for s in (s0, s0 + 1):
+                rows = slice(s * K, (s + 1) * K)
                 spec = both[:, (s - s0) * width : (s - s0 + 1) * width]
-                cross = pltpu.roll(spec, frames, 1) * sign
-                rotated = spec * cosines[:, s : s + 1] + cross * sines[:, s : s + 1]
-                turned[pl.ds(s, K, stride=stations), :] = rotated
-        for k0 in range(0, K, 16):
-            piece = turned[k0 * stations : (k0 + 16) * stations, :].astype(BF16)
-            out[k0 : k0 + 16, r] = piece.reshape(16, stations, width)
-        return carry
-
-    lax.fori_loop(0, RADIX, transform, 0)
+                cross = pltpu.roll(spec, width // 2, 1)
+                rotated = spec * cosines[rows, :] + cross * sines[rows, :]
+                turned[pl.ds(s, K, stride=stations + 1), :] = rotated
+        if r >= 2:
+            sent(r - 2, slot).wait()
+        for k in range(K):
+            top = k * (stations + 1)
+            packed[slot, k] = turned[top : top + stations, :].astype(BF16)
+        sent(r, slot).start()
+    sent(RADIX - 2, 0).wait()
+    sent(RADIX - 1, 1).wait()
+
+
+def rows_of(count):
+    return -(-count // SUB) * SUB
 
 
 def front(delays, voltages, early, late, filter_taps, fringe, fringe_rate):
     stations, samples = voltages.shape[1], voltages.shape[2]
     frames = samples // C
-    blocks = samples // LANES
-    row_step = ROW_PAD + EARLY + blocks + LATE + 1
-    rot_cos, rot_sin = rotation_tables(fringe, fringe_rate)
+    ahead = P_SIZE * (frames // P_SIZE - 1)
+    rest = frames - ahead
+    phases, coarse = rotation_tables(fringe, fringe_rate)
     taps = filter_taps.reshape(P_SIZE * SUB, LANES)
     vmem = pl.BlockSpec(memory_space=pltpu.VMEM)
     smem = pl.BlockSpec(memory_space=pltpu.SMEM)
-    return pl.pallas_call(
-        front_kernel,
-        out_shape=jax.ShapeDtypeStruct((K, RADIX, stations, 2 * frames), BF16),
-        in_specs=[smem] + [vmem] * 7,
+    anywhere = pl.BlockSpec(memory_space=pl.ANY)
+    step = ROW_PAD + EARLY + samples // LANES + 1
+    first = pl.pallas_call(
+        first_kernel,
+        out_shape=jax.ShapeDtypeStruct((RADIX, stations, ahead, 2 * K), BF16),
+        in_specs=[smem, smem, vmem, vmem, vmem],
         out_specs=vmem,
         scratch_shapes=[
-            pltpu.VMEM((-(-(2 * stations * row_step) // 8) * 8, LANES), F32),
-            pltpu.VMEM((2 * stations * frames * SUB, LANES), F32),
-            pltpu.VMEM((RADIX, stations * 2 * frames, 2 * K), BF16),
-            pltpu.VMEM((K * stations, LANES), F32),
+            pltpu.VMEM((rows_of(2 * stations * step), LANES), F32),
+            pltpu.VMEM((2 * stations * ahead * STEP, LANES), F32),
         ],
-        compiler_params=pltpu.CompilerParams(vmem_limit_bytes=56 * 1024 * 1024),
-        name="front",
-    )(delays, voltages, early, late, taps, jnp.asarray(dft_table()), rot_cos, rot_sin)
+        compiler_params=pltpu.CompilerParams(vmem_limit_bytes=36 * 2**20),
+        cost_estimate=pl.CostEstimate(
+            flops=10**10, bytes_accessed=2**23, transcendentals=0
+        ),
+        name="first",
+    )(delays, phases, voltages, early, taps)
+    tail = rest * C + DMAX
+    step = ROW_PAD + tail // LANES + LATE + 1
+    return pl.pallas_call(
+        second_kernel,
+        out_shape=jax.ShapeDtypeStruct((K, RADIX, stations, 2 * frames), BF16),
+        in_specs=[smem, smem, vmem, vmem, vmem, vmem, vmem, vmem],
+        out_specs=anywhere,
+        scratch_shapes=[
+            pltpu.VMEM((rows_of(2 * stations * step), LANES), F32),
+            pltpu.VMEM((2 * stations * rest * STEP, LANES), F32),
+            pltpu.VMEM((RADIX, stations, rest, 2 * K), BF16),
+            pltpu.VMEM((stations * K, 2 * frames), F32),
+            pltpu.VMEM((stations * K, 2 * frames), F32),
+            pltpu.VMEM((K * (stations + 1), 2 * frames), F32),
+            pltpu.VMEM((2, K, stations, 2 * frames), BF16),
+            pltpu.SemaphoreType.DMA((2,)),
+        ],
+        compiler_params=pltpu.CompilerParams(vmem_limit_bytes=40 * 2**20),
+        cost_estimate=pl.CostEstimate(
+            flops=10**10, bytes_accessed=2**23, transcendentals=0
+        ),
+        name="second",
+    )(delays, phases, voltages, late, taps, jnp.asarray(dft_table()), coarse, first)
 
 
 def gram_kernel(scale, groups, times, received, real, imag):

time: 123 us -> 111 us (0.902)
  Pallas kernels: 39.1 us -> 30.9 us
  waiting for transfers between devices: 4.46 us -> 0.01 us
  local copies, waits for them, and re-layouts: 4.01 us -> 6.25 us
  other arithmetic: 3.58 us -> 1.55 us
    pallas_call x1 -> x2, Pallas kernels: 30.9 us -> 22.7 us  [the longest x1 11.5 us: front(): pl.pallas_call(first_kernel, out_shape=jax.ShapeDtypeStruct((RADIX, stati...]
    ppermute x2, waiting for transfers between devices: 4.46 us -> 0.01 us  [from_behind(): return lax.ppermute(block, axis, route)]
    unnamed x7 -> x10, local copies, waits for them, and re-layouts: 0.95 us -> 2.85 us
    mul x2, other arithmetic: 2.8 us -> 1.38 us  [the longest x1 0.72 us: rotation_tables(): jnp.cos(fine) * scale]
  transfers between devices with their start and end apart: 2 -> 2, of which waited for: 1 -> 0; matrix products, arithmetic and copies ran while one was open for 4% -> 4% of each run, Pallas kernels for 0% -> 10%
where the time goes in v2:
time: 111 us
  blocking collectives  65.4 us (59%)
  Pallas kernels  30.9 us (28%)
  local copies, waits for them, and re-layouts  6.25 us (6%)
  starting transfers between devices  5.69 us (5%)
  other arithmetic  1.55 us (1%)
    all_to_all x1, blocking collectives, local(): lax.all_to_all(outgoing, ('stn', 'tm'), split_axis=0, concat_axis=0, tile...  65.4 us
    pallas_call x1, Pallas kernels, front(): pl.pallas_call(first_kernel, out_shape=jax.ShapeDtypeStruct((RADIX, stati...  11.5 us
    pallas_call x1, Pallas kernels, front(): pl.pallas_call(second_kernel, out_shape=jax.ShapeDtypeStruct((K, RADIX, s...  11.2 us
    pallas_call x1, Pallas kernels, gram(): pl.pallas_call(body, grid=(channels,), out_shape=(shape, shape), in_specs...  8.25 us
    ppermute x2, starting transfers between devices, from_behind(): return lax.ppermute(block, axis, route)  5.69 us
    unnamed x10, local copies, waits for them, and re-layouts  2.85 us
  transfers between devices with their start and end apart: 2, of which 0 were waited for; matrix products, arithmetic and copies ran while one was open for 4% of the time, Pallas kernels for 10%

profile of v2, /device:TPU:7, one launch (start us, length us, event | category | flops | bytes accessed | tf_op | source)
XLA Modules:
  0.0 110.5 jit_solution(6001599873038619842)
XLA Ops:
  0.6 0.9 slice.7
  1.5 3.8 %collective-permute-start.1 = (bf16[2,16,2048]{2,1,0:T(8,128)(2,1)S(1)}, bf16[2,16,2048]{2,1,0:T(8,128)(2,1)S(1)}, u32[]{:S(2)}, u32[]{:S(2)}) collective-permute-start(bf16[2,16,2048]{2,1,0:T(8,128)(2,1)S(1)} %slice.7), channel_id=1, source_target_pairs={{0,1},{1,2},{2,3},{4,5},{5,6},{6,7},{8,9},{9,10},{10,11},{12,13},{... | collective-permute-start | bytes 393224 | tf_op jit(solution)/shard_map/ppermute | solution.py:27
  5.3 1.3 %slice.6 = bf16[2,16,15360]{2,1,0:T(8,128)(2,1)S(1)} slice(bf16[2,16,65536]{2,1,0:T(8,128)(2,1)} %volts.3), slice={[0:2], [0:16], [0:15360]} | slice | bytes 1966080 | tf_op jit(solution)/shard_map/slice | solution.py:286
  6.6 1.9 %collective-permute-start = (bf16[2,16,15360]{2,1,0:T(8,128)(2,1)S(1)}, bf16[2,16,15360]{2,1,0:T(8,128)(2,1)S(1)}, u32[]{:S(2)}, u32[]{:S(2)}) collective-permute-start(bf16[2,16,15360]{2,1,0:T(8,128)(2,1)S(1)} %slice.6), channel_id=1, source_target_pairs={{1,0},{2,1},{3,2},{5,4},{6,5},{7,6},{9,8},{10,9},{11,10},{13,12},{... | collective-permute-start | bytes 2949128 | tf_op jit(solution)/shard_map/ppermute | solution.py:27
  8.5 0.7 broadcast_multiply_fusion
  9.2 0.7 cosine_multiply_fusion
  9.9 0.2 fusion.7
  10.1 0.1 copy.8
  10.2 0.1 reshape.165.phases
  10.3 0.9 reshape.166.taps
  11.2 0.1 copy.9
  11.3 0.0 collective-permute-done.1.early
  11.3 0.0 copy-start
  11.3 2.2 %copy-done = bf16[2,16,65536]{2,1,0:T(8,128)(2,1)S(1)} copy-done((bf16[2,16,65536]{2,1,0:T(8,128)(2,1)S(1)}, bf16[2,16,65536]{2,1,0:T(8,128)(2,1)}, u32[]{:S(2)}) %copy-start) | copy-done | bytes 4194328
  13.5 0.0 copy-start.2
  13.5 0.7 copy-done.2
  14.2 0.0 copy-start.1
  14.2 0.0 copy-start.3
  14.2 0.0 copy-start.4
  14.2 11.5 %first.1.before = bf16[4,16,48,512]{3,2,1,0:T(8,128)(2,1)S(1)} custom-call(s32[16]{0:T(128)S(1)} %copy-done.2, f32[128]{0:T(128)S(1)} %reshape.165.phases, bf16[2,16,65536]{2,1,0:T(8,128)(2,1)S(1)} %copy-done, bf16[2,16,2048]{2,1,0:T(8,128)(2,1)S(1)} %collective-permute-done.1.early, f32[128,128]{1,0:T(8,128)S(1)} %reshape.166.taps), custom_call_target="tpu_custom_call" | custom-call | flops 10000000000 | bytes 8388608 | tf_op jit(solution)/shard_map/first/pallas_call | solution.py:204
  25.7 0.0 collective-permute-done.late
  25.7 0.0 copy-done.1
  25.7 0.0 copy-done.3
  25.7 0.0 copy-done.4
  25.7 11.2 %second.1 = bf16[256,4,16,128]{3,2,1,0:T(8,128)(2,1)S(1)} custom-call(s32[16]{0:T(128)S(1)} %copy-done.3, f32[128]{0:T(128)S(1)} %reshape.165.phases, bf16[2,16,65536]{2,1,0:T(8,128)(2,1)S(1)} %copy-done.1, bf16[2,16,15360]{2,1,0:T(8,128)(2,1)S(1)} %collective-permute-done.late, f32[128,128]{1,0:T(8,128)S(1)} %reshape.166.taps, ...), custom_call_target="tpu_custom_call" | custom-call | flops 10000000000 | bytes 8388608 | tf_op jit(solution)/shard_map/second/pallas_call | solution.py:221
  36.9 65.4 %all_to_all.5.received = bf16[128,8,16,128]{3,2,1,0:T(8,128)(2,1)S(1)} all-to-all(bf16[128,8,16,128]{3,2,1,0:T(8,128)(2,1)S(1)} %bitcast.2), channel_id=1, replica_groups=mesh['stn'=32,'tm'=4] {'stn','tm'}, dimensions={0} | all-to-all | bytes 8388608 | tf_op jit(solution)/shard_map/all_to_all | solution.py:291
  102.3 8.2 %gram.1 = (f32[8,512,512]{2,1,0:T(8,128)}, f32[8,512,512]{2,1,0:T(8,128)}) custom-call(bf16[128,8,16,128]{3,2,1,0:T(8,128)(2,1)S(1)} %all_to_all.5.received), custom_call_target="tpu_custom_call" | custom-call | tf_op jit(solution)/shard_map/gram/pallas_call | solution.py:270
  (2 shorter events, 0.0 us)
Async XLA Ops:
  1.5 9.8 %collective-permute-start.1 = (bf16[2,16,2048]{2,1,0:T(8,128)(2,1)S(1)}, bf16[2,16,2048]{2,1,0:T(8,128)(2,1)S(1)}, u32[]{:S(2)}, u32[]{:S(2)}) collective-permute-start(bf16[2,16,2048]{2,1,0:T(8,128)(2,1)S(1)} %slice.7), channel_id=1, source_target_pairs={{0,1},{1,2},{2,3},{4,5},{5,6},{6,7},{8,9},{9,10},{10,11},{12,13},{... | collective-permute-start | bytes 393224 | tf_op jit(solution)/shard_map/ppermute | solution.py:27
  6.6 19.1 %collective-permute-start = (bf16[2,16,15360]{2,1,0:T(8,128)(2,1)S(1)}, bf16[2,16,15360]{2,1,0:T(8,128)(2,1)S(1)}, u32[]{:S(2)}, u32[]{:S(2)}) collective-permute-start(bf16[2,16,15360]{2,1,0:T(8,128)(2,1)S(1)} %slice.6), channel_id=1, source_target_pairs={{1,0},{2,1},{3,2},{5,4},{6,5},{7,6},{9,8},{10,9},{11,10},{13,12},{... | collective-permute-start | bytes 2949128 | tf_op jit(solution)/shard_map/ppermute | solution.py:27
  11.3 2.2 %copy-start = (bf16[2,16,65536]{2,1,0:T(8,128)(2,1)S(1)}, bf16[2,16,65536]{2,1,0:T(8,128)(2,1)}, u32[]{:S(2)}) copy-start(bf16[2,16,65536]{2,1,0:T(8,128)(2,1)} %volts.3) | copy-start | bytes 12582916
  13.5 0.7 copy-start.2
  14.2 11.5 %copy-start.1 = (bf16[2,16,65536]{2,1,0:T(8,128)(2,1)S(1)}, bf16[2,16,65536]{2,1,0:T(8,128)(2,1)}, u32[]{:S(2)}) copy-start(bf16[2,16,65536]{2,1,0:T(8,128)(2,1)} %volts.3) | copy-start | bytes 12582916
  14.2 11.5 %copy-start.3 = (s32[16]{0:T(128)S(1)}, s32[16]{0:T(128)}, u32[]{:S(2)}) copy-start(s32[16]{0:T(128)} %delays.3) | copy-start | bytes 196
  14.2 11.5 %copy-start.4 = (bf16[1024,512]{1,0:T(8,128)(2,1)S(1)}, bf16[1024,512]{1,0:T(8,128)(2,1)}, u32[]{:S(2)}) copy-start(bf16[1024,512]{1,0:T(8,128)(2,1)} %constant.32.clone.table) | copy-start | bytes 3145732

commit v3 on v2

--- a/solution.py
+++ b/solution.py
@@ -33,21 +33,38 @@
     return np.concatenate([np.cos(angle), np.sin(angle)], axis=1).astype(BF16)
 
 
-def rotation_tables(fringe, fringe_rate):
-    fine = (fringe[:, None] + fringe_rate[:, None] * jnp.arange(RADIX)[None, :]) % Q
-    fine = fine.astype(F32) * (TWO_PI / Q)
-    scale = 1.0 / math.sqrt(C)
-    phases = jnp.stack([jnp.cos(fine) * scale, jnp.sin(fine) * scale], axis=2).reshape(-1)
-    coarse = (RADIX * fringe_rate[:, None] * jnp.arange(K)[None, :]) % Q
-    coarse = coarse.astype(F32) * (TWO_PI / Q)
-    coarse = lax.optimization_barrier(jnp.concatenate([jnp.cos(coarse), jnp.sin(coarse)]))
-    return phases, coarse.T
-
-
 EARLY = DMAX // LANES
 LATE = (P_SIZE - 1) * C // LANES
 ROW_PAD = 8
 STEP = SUB + 1
+
+
+def phase_rows(fringe, fringe_rate, stations, phases):
+    row = lax.broadcasted_iota(jnp.int32, (SUB, LANES), 0)
+    turn = (row & 1).astype(F32) * (math.pi / 2)
+    for s in range(stations):
+        phase = (fringe[s] + fringe_rate[s] * (row >> 1)) & (Q - 1)
+        angle = phase.astype(F32) * (TWO_PI / Q) - turn
+        phases[s * SUB : (s + 1) * SUB, :] = jnp.cos(angle) * (1.0 / math.sqrt(C))
+
+
+def coarse_columns(fringe_rate, stations):
+    row = lax.broadcasted_iota(jnp.int32, (2 * stations, K), 0)
+    k = lax.broadcasted_iota(jnp.int32, (2 * stations, K), 1)
+    rate = jnp.zeros((2 * stations, K), jnp.int32)
+    for s in range(stations):
+        rate = jnp.where(row % stations == s, fringe_rate[s], rate)
+    angle = ((RADIX * rate * k) & (Q - 1)).astype(F32) * (TWO_PI / Q)
+    values = jnp.cos(angle - jnp.where(row < stations, 0.0, math.pi / 2))
+    padding = jnp.zeros((LANES - 2 * stations, K), F32)
+    return jnp.concatenate([values, padding], axis=0).T
+
+
+def tap_rows(filter_taps, taps):
+    for p in range(P_SIZE):
+        for j in range(SUB):
+            row = p * SUB + j
+            taps[row : row + 1, :] = filter_taps[p : p + 1, j * LANES : (j + 1) * LANES]
 
 
 def spread(source, first, count, offset, stations, row_step, lin):
@@ -93,7 +110,7 @@
     lax.fori_loop(0, 2 * stations, filter_row, 0, unroll=2)
 
 
-def butterflies(phases, stations, frames, filt, zs):
+def butterflies(phases, stations, frames, filt, zs, top=0):
     def body(s, carry):
         def load(part, j):
             start = (part * stations + s) * (frames * STEP) + j
@@ -113,45 +130,71 @@
                 (re_d - im_g, im_d + re_g),
             ]
             for r in range(RADIX):
-                cosine = phases[(s * RADIX + r) * 2]
-                sine = phases[(s * RADIX + r) * 2 + 1]
+                cosine = phases[pl.ds(s * SUB + 2 * r, 1), :]
+                sine = phases[pl.ds(s * SUB + 2 * r + 1, 1), :]
                 zr = z[r][0] * cosine - z[r][1] * sine
                 zi = z[r][0] * sine + z[r][1] * cosine
-                zs[r, s, :, pl.ds(half * LANES, LANES)] = zr.astype(BF16)
-                zs[r, s, :, pl.ds(K + half * LANES, LANES)] = zi.astype(BF16)
+                zs[r, s, top : top + frames, pl.ds(half * LANES, LANES)] = zr.astype(BF16)
+                zs[r, s, top : top + frames, pl.ds(K + half * LANES, LANES)] = zi.astype(BF16)
         return carry
 
     lax.fori_loop(0, stations, body, 0)
 
 
-def first_kernel(delays, phases, volts, early, taps, zs, lin, filt):
-    stations, samples = volts.shape[1], volts.shape[2]
+def rims_kernel(volts, early, late, sems):
+    samples = volts.shape[2]
+    size = early.shape[2]
+    copies = [
+        pltpu.make_async_copy(
+            volts.at[:, :, pl.ds(0, late.shape[2])], late, sems.at[0]
+        ),
+        pltpu.make_async_copy(
+            volts.at[:, :, pl.ds(samples - size, size)], early, sems.at[1]
+        ),
+    ]
+    for copy in copies:
+        copy.start()
+    for copy in copies:
+        copy.wait()
+
+
+def first_kernel(
+    delays, fringe, fringe_rate, volts, filter_taps, zs, phases, coarse, taps, lin, filt
+):
+    stations = volts.shape[1]
     frames = zs.shape[2]
     row_step = lin.shape[0] // (2 * stations)
-    spread(early, 0, EARLY, 0, stations, row_step, lin)
-    spread(volts, 0, samples // LANES, EARLY, stations, row_step, lin)
+    phase_rows(fringe, fringe_rate, stations, phases)
+    coarse[...] = coarse_columns(fringe_rate, stations)
+    tap_rows(filter_taps, taps)
+    blocks = (frames + P_SIZE - 1) * SUB + EARLY
+    spread(volts, P_SIZE * SUB - EARLY, blocks, 0, stations, row_step, lin)
     filter_frames(delays, taps, stations, frames, row_step, lin, filt)
     butterflies(phases, stations, frames, filt, zs)
 
 
 def second_kernel(
-    delays, phases, volts, late, taps, table, coarse, before, out,
+    delays, volts, early, late, taps, table, phases, coarse, before, out,
     lin, filt, zs, cosines, sines, turned, packed, sems
 ):
-    stations = volts.shape[1]
-    done, frames = before.shape[2], zs.shape[2]
-    width = 2 * (done + frames)
+    stations, blocks = volts.shape[1], volts.shape[2] // LANES
+    frames = zs.shape[2]
+    width = 2 * (before.shape[2] + frames)
     row_step = lin.shape[0] // (2 * stations)
     sign = jnp.where(lax.broadcasted_iota(jnp.int32, (1, width), 1) < width // 2, -1.0, 1.0)
     for s in range(stations):
         rows = slice(s * K, (s + 1) * K)
         cosines[rows, :] = jnp.broadcast_to(coarse[:, s : s + 1], (K, width))
         sines[rows, :] = coarse[:, stations + s : stations + s + 1] * sign
-    blocks = frames * C // LANES + EARLY
-    spread(volts, volts.shape[2] // LANES - blocks, blocks, 0, stations, row_step, lin)
-    spread(late, 0, LATE, blocks, stations, row_step, lin)
-    filter_frames(delays, taps, stations, frames, row_step, lin, filt)
-    butterflies(phases, stations, frames, filt, zs)
+    spread(early, 0, EARLY, 0, stations, row_step, lin)
+    spread(volts, 0, (2 * P_SIZE - 1) * SUB, EARLY, stations, row_step, lin)
+    filter_frames(delays, taps, stations, P_SIZE, row_step, lin, filt)
+    butterflies(phases, stations, P_SIZE, filt, zs)
+    own = P_SIZE * SUB + EARLY
+    spread(volts, blocks - own, own, 0, stations, row_step, lin)
+    spread(late, 0, LATE, own, stations, row_step, lin)
+    filter_frames(delays, taps, stations, P_SIZE, row_step, lin, filt)
+    butterflies(phases, stations, P_SIZE, filt, zs, P_SIZE)
 
     def sent(r, slot):
         return pltpu.make_async_copy(packed.at[slot], out.at[:, r], sems.at[slot])
@@ -190,42 +233,57 @@
     return -(-count // SUB) * SUB
 
 
-def front(delays, voltages, early, late, filter_taps, fringe, fringe_rate):
+def front(voltages, delays, fringe, fringe_rate, filter_taps):
     stations, samples = voltages.shape[1], voltages.shape[2]
     frames = samples // C
-    ahead = P_SIZE * (frames // P_SIZE - 1)
-    rest = frames - ahead
-    phases, coarse = rotation_tables(fringe, fringe_rate)
-    taps = filter_taps.reshape(P_SIZE * SUB, LANES)
+    rest = 2 * P_SIZE
+    ahead = frames - rest
     vmem = pl.BlockSpec(memory_space=pltpu.VMEM)
     smem = pl.BlockSpec(memory_space=pltpu.SMEM)
     anywhere = pl.BlockSpec(memory_space=pl.ANY)
-    step = ROW_PAD + EARLY + samples // LANES + 1
-    first = pl.pallas_call(
+    estimate = pl.CostEstimate(flops=10**10, bytes_accessed=2**23, transcendentals=0)
+    early, late = pl.pallas_call(
+        rims_kernel,
+        out_shape=[
+            jax.ShapeDtypeStruct((2, stations, DMAX), BF16),
+            jax.ShapeDtypeStruct((2, stations, (P_SIZE - 1) * C), BF16),
+        ],
+        in_specs=[anywhere],
+        out_specs=[vmem, vmem],
+        scratch_shapes=[pltpu.SemaphoreType.DMA((2,))],
+        compiler_params=pltpu.CompilerParams(vmem_limit_bytes=57 * 2**20),
+        name="rims",
+    )(voltages)
+    late = from_behind(late, "tm", -1)
+    early = from_behind(early, "tm", 1)
+    step = ROW_PAD + EARLY + (ahead + P_SIZE - 1) * SUB + 1
+    before, phases, coarse, taps = pl.pallas_call(
         first_kernel,
-        out_shape=jax.ShapeDtypeStruct((RADIX, stations, ahead, 2 * K), BF16),
-        in_specs=[smem, smem, vmem, vmem, vmem],
-        out_specs=vmem,
+        out_shape=[
+            jax.ShapeDtypeStruct((RADIX, stations, ahead, 2 * K), BF16),
+            jax.ShapeDtypeStruct((stations * SUB, LANES), F32),
+            jax.ShapeDtypeStruct((K, LANES), F32),
+            jax.ShapeDtypeStruct((P_SIZE * SUB, LANES), F32),
+        ],
+        in_specs=[smem, smem, smem, vmem, vmem],
+        out_specs=[vmem] * 4,
         scratch_shapes=[
             pltpu.VMEM((rows_of(2 * stations * step), LANES), F32),
             pltpu.VMEM((2 * stations * ahead * STEP, LANES), F32),
         ],
-        compiler_params=pltpu.CompilerParams(vmem_limit_bytes=36 * 2**20),
-        cost_estimate=pl.CostEstimate(
-            flops=10**10, bytes_accessed=2**23, transcendentals=0
-        ),
+        compiler_params=pltpu.CompilerParams(vmem_limit_bytes=28 * 2**20),
+        cost_estimate=estimate,
         name="first",
-    )(delays, phases, voltages, early, taps)
-    tail = rest * C + DMAX
-    step = ROW_PAD + tail // LANES + LATE + 1
+    )(delays, fringe, fringe_rate, voltages, filter_taps)
+    step = ROW_PAD + EARLY + (2 * P_SIZE - 1) * SUB + 1
     return pl.pallas_call(
         second_kernel,
         out_shape=jax.ShapeDtypeStruct((K, RADIX, stations, 2 * frames), BF16),
-        in_specs=[smem, smem, vmem, vmem, vmem, vmem, vmem, vmem],
+        in_specs=[smem] + [vmem] * 8,
         out_specs=anywhere,
         scratch_shapes=[
             pltpu.VMEM((rows_of(2 * stations * step), LANES), F32),
-            pltpu.VMEM((2 * stations * rest * STEP, LANES), F32),
+            pltpu.VMEM((2 * stations * P_SIZE * STEP, LANES), F32),
             pltpu.VMEM((RADIX, stations, rest, 2 * K), BF16),
             pltpu.VMEM((stations * K, 2 * frames), F32),
             pltpu.VMEM((stations * K, 2 * frames), F32),
@@ -234,11 +292,11 @@
             pltpu.SemaphoreType.DMA((2,)),
         ],
         compiler_params=pltpu.CompilerParams(vmem_limit_bytes=40 * 2**20),
-        cost_estimate=pl.CostEstimate(
-            flops=10**10, bytes_accessed=2**23, transcendentals=0
-        ),
+        cost_estimate=estimate,
         name="second",
-    )(delays, phases, voltages, late, taps, jnp.asarray(dft_table()), coarse, first)
+    )(
+        delays, voltages, early, late, taps, jnp.asarray(dft_table()), phases, coarse, before
+    )
 
 
 def gram_kernel(scale, groups, times, received, real, imag):
@@ -282,9 +340,7 @@
     samples = voltages.shape[2]
     stations = voltages.shape[1]
     frames = samples // C
-    early = from_behind(voltages[:, :, samples - DMAX :], "tm", 1)
-    late = from_behind(voltages[:, :, : (P_SIZE - 1) * C], "tm", -1)
-    turned = front(delays, voltages, early, late, filter_taps, fringe, fringe_rate)
+    turned = front(voltages, delays, fringe, fringe_rate, filter_taps)
     groups, times = lax.axis_size("stn"), lax.axis_size("tm")
     devices = groups * times
     outgoing = turned.reshape(devices, C // devices, stations, 2 * frames)

time: 111 us -> 109 us (0.982)
  local copies, waits for them, and re-layouts: 6.25 us -> 0.86 us
  Pallas kernels: 30.9 us -> 35.5 us
  other arithmetic: 1.55 us -> 0 us
    pallas_call x1, Pallas kernels: 11.2 us -> 16.3 us  [front(): pl.pallas_call(second_kernel, out_shape=jax.ShapeDtypeStruct((K, RADIX, s...]
    slice x2 -> x0, local copies, waits for them, and re-layouts: 2.18 us -> none  [the longest x1 1.27 us: local(): late = from_behind(voltages[:, :, :(P_SIZE - 1) * C], 'tm', -1)]
    unnamed x10 -> x12, local copies, waits for them, and re-layouts: 2.85 us -> 0.86 us
    mul x2 -> x0, other arithmetic: 1.38 us -> none  [the longest x1 0.72 us: rotation_tables(): jnp.cos(fine) * scale]
    pallas_call x1 -> x2, Pallas kernels: 11.5 us -> 11 us  [the longest x1 8.65 us: front(): pl.pallas_call(first_kernel, out_shape=[jax.ShapeDtypeStruct((RADIX, stat...]
  transfers between devices with their start and end apart: 2 -> 2, of which waited for: 0 -> 1; matrix products, arithmetic and copies ran while one was open for 4% -> 0% of each run, Pallas kernels for 10% -> 8%
where the time goes in v3:
time: 109 us; the launch traced here: 108 us
  blocking collectives  65 us (60%)
  Pallas kernels  35.5 us (33%)
  starting transfers between devices  5.68 us (5%)
    all_to_all x1, blocking collectives, local(): lax.all_to_all(outgoing, ('stn', 'tm'), split_axis=0, concat_axis=0, tile...  65 us
    pallas_call x1, Pallas kernels, front(): pl.pallas_call(second_kernel, out_shape=jax.ShapeDtypeStruct((K, RADIX, s...  16.3 us
    pallas_call x1, Pallas kernels, front(): pl.pallas_call(first_kernel, out_shape=[jax.ShapeDtypeStruct((RADIX, stat...  8.65 us
    pallas_call x1, Pallas kernels, gram(): pl.pallas_call(body, grid=(channels,), out_shape=(shape, shape), in_specs...  8.25 us
    ppermute x2, starting transfers between devices, from_behind(): return lax.ppermute(block, axis, route)  5.68 us
    pallas_call x1, Pallas kernels, front(): pl.pallas_call(rims_kernel, out_shape=[jax.ShapeDtypeStruct((2, stations,...  2.36 us
  transfers between devices with their start and end apart: 2, of which 1 were waited for; matrix products, arithmetic and copies ran while one was open for 0% of the time, Pallas kernels for 8%

profile of v3, /device:TPU:7, one launch (start us, length us, event | category | flops | bytes accessed | tf_op | source)
XLA Modules:
  0.0 108.3 jit_solution(4503141110449092620)
XLA Ops:
  0.6 0.0 copy-start
  0.6 0.0 copy-start.4
  0.7 0.0 copy-start.3
  0.7 0.0 copy-start.2
  0.7 2.4 %rims.1 = (bf16[2,16,2048]{2,1,0:T(8,128)(2,1)}, bf16[2,16,15360]{2,1,0:T(8,128)(2,1)}) custom-call(bf16[2,16,65536]{2,1,0:T(8,128)(2,1)} %volts.5), custom_call_target="tpu_custom_call" | custom-call | tf_op jit(solution)/shard_map/rims/pallas_call | solution.py:245
  3.0 2.6 %collective-permute-start.1 = (bf16[2,16,15360]{2,1,0:T(8,128)(2,1)}, bf16[2,16,15360]{2,1,0:T(8,128)(2,1)S(1)}, u32[]{:S(2)}, u32[]{:S(2)}) collective-permute-start(bf16[2,16,15360]{2,1,0:T(8,128)(2,1)} %get-tuple-element.9), channel_id=1, source_target_pairs={{1,0},{2,1},{3,2},{5,4},{6,5},{7,6},{9,8},{10,9},{11,10},{13,12},{... | collective-permute-start | bytes 2949128 | tf_op jit(solution)/shard_map/ppermute | solution.py:27
  5.6 3.1 %collective-permute-start = (bf16[2,16,2048]{2,1,0:T(8,128)(2,1)}, bf16[2,16,2048]{2,1,0:T(8,128)(2,1)S(1)}, u32[]{:S(2)}, u32[]{:S(2)}) collective-permute-start(bf16[2,16,2048]{2,1,0:T(8,128)(2,1)} %get-tuple-element.8), channel_id=1, source_target_pairs={{0,1},{1,2},{2,3},{4,5},{5,6},{6,7},{8,9},{9,10},{10,11},{12,13},{... | collective-permute-start | bytes 393224 | tf_op jit(solution)/shard_map/ppermute | solution.py:27
  8.7 0.0 copy-done
  8.7 0.0 copy-done.4
  8.8 0.0 copy-done.3
  8.8 0.0 copy-done.2
  8.8 0.0 copy-start.1
  8.8 0.8 copy-done.1
  9.6 0.0 copy-start.5
  9.6 8.7 %first.1 = (bf16[4,16,32,512]{3,2,1,0:T(8,128)(2,1)S(1)}, f32[128,128]{1,0:T(8,128)S(1)}, f32[256,128]{1,0:T(8,128)S(1)}, f32[128,128]{1,0:T(8,128)S(1)}) custom-call(s32[16]{0:T(128)S(1)} %copy-done.4, s32[16]{0:T(128)S(1)} %copy-done.2, s32[16]{0:T(128)S(1)} %copy-done.3, bf16[2,16,65536]{2,1,0:T(8,128)(2,1)S(1)} %copy-done, f32[16,1024]{1,0:T(8,128)S(1)} %copy-done.1), custom_call_target="tpu_custom_call" | custom-call | flops 10000000000 | bytes 8388608 | tf_op jit(solution)/shard_map/first/pallas_call | solution.py:260
  18.3 0.0 collective-permute-done.early
  18.3 0.5 collective-permute-done.1.late
  18.8 0.0 copy-done.5
  18.8 16.3 %second.1 = bf16[256,4,16,128]{3,2,1,0:T(8,128)(2,1)S(1)} custom-call(s32[16]{0:T(128)S(1)} %copy-done.4, bf16[2,16,65536]{2,1,0:T(8,128)(2,1)S(1)} %copy-done, bf16[2,16,2048]{2,1,0:T(8,128)(2,1)S(1)} %collective-permute-done.early, bf16[2,16,15360]{2,1,0:T(8,128)(2,1)S(1)} %collective-permute-done.1.late, f32[128,128]{1,0:T(8,128)S(1)} %get-tuple-element.10.taps, ...), custom_call_target="tpu_custom_call" | custom-call | flops 10000000000 | bytes 8388608 | tf_op jit(solution)/shard_map/second/pallas_call | solution.py:279
  35.1 65.0 %all_to_all.5.received = bf16[128,8,16,128]{3,2,1,0:T(8,128)(2,1)S(1)} all-to-all(bf16[128,8,16,128]{3,2,1,0:T(8,128)(2,1)S(1)} %bitcast.1), channel_id=1, replica_groups=mesh['stn'=32,'tm'=4] {'stn','tm'}, dimensions={0} | all-to-all | bytes 8388608 | tf_op jit(solution)/shard_map/all_to_all | solution.py:347
  100.1 8.2 %gram.1 = (f32[8,512,512]{2,1,0:T(8,128)}, f32[8,512,512]{2,1,0:T(8,128)}) custom-call(bf16[128,8,16,128]{3,2,1,0:T(8,128)(2,1)S(1)} %all_to_all.5.received), custom_call_target="tpu_custom_call" | custom-call | tf_op jit(solution)/shard_map/gram/pallas_call | solution.py:328
Async XLA Ops:
  0.6 8.1 %copy-start = (bf16[2,16,65536]{2,1,0:T(8,128)(2,1)S(1)}, bf16[2,16,65536]{2,1,0:T(8,128)(2,1)}, u32[]{:S(2)}) copy-start(bf16[2,16,65536]{2,1,0:T(8,128)(2,1)} %volts.5) | copy-start | bytes 12582916
  0.6 8.1 %copy-start.4 = (s32[16]{0:T(128)S(1)}, s32[16]{0:T(128)}, u32[]{:S(2)}) copy-start(s32[16]{0:T(128)} %delays.3) | copy-start | bytes 196
  0.7 8.1 %copy-start.3 = (s32[16]{0:T(128)S(1)}, s32[16]{0:T(128)}, u32[]{:S(2)}) copy-start(s32[16]{0:T(128)} %fringe_rate.1) | copy-start | bytes 196
  0.7 8.1 %copy-start.2 = (s32[16]{0:T(128)S(1)}, s32[16]{0:T(128)}, u32[]{:S(2)}) copy-start(s32[16]{0:T(128)} %fringe.1) | copy-start | bytes 196
  3.0 15.7 %collective-permute-start.1 = (bf16[2,16,15360]{2,1,0:T(8,128)(2,1)}, bf16[2,16,15360]{2,1,0:T(8,128)(2,1)S(1)}, u32[]{:S(2)}, u32[]{:S(2)}) collective-permute-start(bf16[2,16,15360]{2,1,0:T(8,128)(2,1)} %get-tuple-element.9), channel_id=1, source_target_pairs={{1,0},{2,1},{3,2},{5,4},{6,5},{7,6},{9,8},{10,9},{11,10},{13,12},{... | collective-permute-start | bytes 2949128 | tf_op jit(solution)/shard_map/ppermute | solution.py:27
  5.6 12.7 %collective-permute-start = (bf16[2,16,2048]{2,1,0:T(8,128)(2,1)}, bf16[2,16,2048]{2,1,0:T(8,128)(2,1)S(1)}, u32[]{:S(2)}, u32[]{:S(2)}) collective-permute-start(bf16[2,16,2048]{2,1,0:T(8,128)(2,1)} %get-tuple-element.8), channel_id=1, source_target_pairs={{0,1},{1,2},{2,3},{4,5},{5,6},{6,7},{8,9},{9,10},{10,11},{12,13},{... | collective-permute-start | bytes 393224 | tf_op jit(solution)/shard_map/ppermute | solution.py:27
  8.8 0.8 copy-start.1
  9.6 9.2 %copy-start.5 = (bf16[1024,512]{1,0:T(8,128)(2,1)S(1)}, bf16[1024,512]{1,0:T(8,128)(2,1)}, u32[]{:S(2)}) copy-start(bf16[1024,512]{1,0:T(8,128)(2,1)} %constant.2.clone.table) | copy-start | bytes 3145732

commit v4 on v3

--- a/solution.py
+++ b/solution.py
@@ -28,43 +28,57 @@
 
 
 def dft_table():
-    channel = (RADIX * np.arange(K)[None, :] + np.arange(RADIX)[:, None]).reshape(C)
-    angle = (channel[:, None] * np.arange(K)[None, :] % C) * (TWO_PI / C)
-    return np.concatenate([np.cos(angle), np.sin(angle)], axis=1).astype(BF16)
+    k, n = np.arange(K)[:, None], np.arange(K)[None, :]
+    blocks = []
+    for g in range(RADIX):
+        angle = ((RADIX * n - g) * k % C) * (TWO_PI / C)
+        blocks.append(np.concatenate([np.cos(angle), np.sin(angle)], axis=1))
+    return np.concatenate(blocks).astype(BF16)
 
 
 EARLY = DMAX // LANES
 LATE = (P_SIZE - 1) * C // LANES
-ROW_PAD = 8
+ROW_PAD = 16
+ROW_END = 9
 STEP = SUB + 1
 
 
 def phase_rows(fringe, fringe_rate, stations, phases):
     row = lax.broadcasted_iota(jnp.int32, (SUB, LANES), 0)
+    lane = lax.broadcasted_iota(jnp.int32, (SUB, LANES), 1)
     turn = (row & 1).astype(F32) * (math.pi / 2)
     for s in range(stations):
-        phase = (fringe[s] + fringe_rate[s] * (row >> 1)) & (Q - 1)
-        angle = phase.astype(F32) * (TWO_PI / Q) - turn
-        phases[s * SUB : (s + 1) * SUB, :] = jnp.cos(angle) * (1.0 / math.sqrt(C))
-
-
-def coarse_columns(fringe_rate, stations):
-    row = lax.broadcasted_iota(jnp.int32, (2 * stations, K), 0)
-    k = lax.broadcasted_iota(jnp.int32, (2 * stations, K), 1)
-    rate = jnp.zeros((2 * stations, K), jnp.int32)
-    for s in range(stations):
-        rate = jnp.where(row % stations == s, fringe_rate[s], rate)
-    angle = ((RADIX * rate * k) & (Q - 1)).astype(F32) * (TWO_PI / Q)
-    values = jnp.cos(angle - jnp.where(row < stations, 0.0, math.pi / 2))
-    padding = jnp.zeros((LANES - 2 * stations, K), F32)
-    return jnp.concatenate([values, padding], axis=0).T
-
-
-def tap_rows(filter_taps, taps):
+        rest = fringe_rate[s] & (RADIX - 1)
+        for half in range(K // LANES):
+            sample = lane + half * LANES
+            phase = (fringe[s] + (rest - RADIX * sample) * (row >> 1)) & (Q - 1)
+            angle = phase.astype(F32) * (TWO_PI / Q) - turn
+            top = (half * stations + s) * SUB
+            phases[top : top + SUB, :] = jnp.cos(angle) * (1.0 / math.sqrt(C))
+
+
+def tap_rows(filter_taps, fringe_rate, stations, pair, taps):
     for p in range(P_SIZE):
         for j in range(SUB):
-            row = p * SUB + j
-            taps[row : row + 1, :] = filter_taps[p : p + 1, j * LANES : (j + 1) * LANES]
+            piece = filter_taps[p : p + 1, j * LANES : (j + 1) * LANES]
+            for copy in range(2):
+                row = SUB + (2 * p + copy) * SUB + j
+                pair[row : row + 1, :] = piece
+    lane = lax.broadcasted_iota(jnp.int32, (SUB, LANES), 1)
+
+    def body(s, carry):
+        delta = -(fringe_rate[s] >> 2)
+        shift = delta & (LANES - 1)
+        keep = lane < LANES - shift
+        for p in range(P_SIZE):
+            base = SUB + 2 * p * SUB - (delta >> 7)
+            here = pair[pl.ds(base, SUB), :]
+            before = pair[pl.ds(base - 1, SUB), :]
+            top = pl.multiple_of(s * (P_SIZE * SUB), SUB) + p * SUB
+            taps[pl.ds(top, SUB), :] = pltpu.roll(jnp.where(keep, here, before), shift, 1)
+        return carry
+
+    lax.fori_loop(0, stations, body, 0)
 
 
 def spread(source, first, count, offset, stations, row_step, lin):
@@ -84,23 +98,35 @@
     lax.fori_loop(0, count // unroll, body, 0)
 
 
-def filter_frames(delays, taps, stations, frames, row_step, lin, filt):
+def filter_frames(delays, fringe_rate, taps, stations, frames, row_step, lin, filt):
     lane = lax.broadcasted_iota(jnp.int32, (SUB, LANES), 1)
+    flat = lax.broadcasted_iota(jnp.int32, (SUB, LANES), 0) * LANES + lane
 
     def filter_row(row, carry):
-        delay = delays[row % stations]
-        shift = delay % LANES
-        base = row * row_step + ROW_PAD + EARLY - delay // LANES
+        s = row % stations
+        moved = fringe_rate[s] >> 2
+        delta = delays[s] - moved
+        shift = delta & (LANES - 1)
+        base = row * row_step + ROW_PAD + EARLY - (delta >> 7)
         keep = lane < LANES - shift
-        sums = {}
-        for k in range(frames + P_SIZE - 1):
+        inner = flat < C - moved
+        top = pl.multiple_of(s * (P_SIZE * SUB), SUB)
+
+        def shifted(k):
             here = lin[pl.ds(base + SUB * k, SUB), :]
             before = lin[pl.ds(base + SUB * k - 1, SUB), :]
-            frame = pltpu.roll(jnp.where(keep, here, before), shift, 1)
+            return pltpu.roll(jnp.where(keep, here, before), shift, 1)
+
+        sums = {}
+        last = shifted(-1)
+        for k in range(frames + P_SIZE - 1):
+            now = shifted(k)
+            frame = jnp.where(inner, now, last)
+            last = now
             for p in range(P_SIZE):
                 m = k - p
                 if 0 <= m < frames:
-                    term = taps[SUB * p : SUB * (p + 1), :] * frame
+                    term = taps[pl.ds(top + SUB * p, SUB), :] * frame
                     sums[m] = sums[m] + term if m in sums else term
             m = k - (P_SIZE - 1)
             if m >= 0:
@@ -130,12 +156,12 @@
                 (re_d - im_g, im_d + re_g),
             ]
             for r in range(RADIX):
-                cosine = phases[pl.ds(s * SUB + 2 * r, 1), :]
-                sine = phases[pl.ds(s * SUB + 2 * r + 1, 1), :]
+                cosine = phases[pl.ds((half * stations + s) * SUB + 2 * r, 1), :]
+                sine = phases[pl.ds((half * stations + s) * SUB + 2 * r + 1, 1), :]
                 zr = z[r][0] * cosine - z[r][1] * sine
                 zi = z[r][0] * sine + z[r][1] * cosine
-                zs[r, s, top : top + frames, pl.ds(half * LANES, LANES)] = zr.astype(BF16)
-                zs[r, s, top : top + frames, pl.ds(K + half * LANES, LANES)] = zi.astype(BF16)
+                zs[s, r, top : top + frames, pl.ds(half * LANES, LANES)] = zr.astype(BF16)
+                zs[s, r, top : top + frames, pl.ds(K + half * LANES, LANES)] = zi.astype(BF16)
         return carry
 
     lax.fori_loop(0, stations, body, 0)
@@ -159,74 +185,57 @@
 
 
 def first_kernel(
-    delays, fringe, fringe_rate, volts, filter_taps, zs, phases, coarse, taps, lin, filt
+    delays, fringe, fringe_rate, volts, filter_taps, zs, phases, taps, pair, lin, filt
 ):
     stations = volts.shape[1]
     frames = zs.shape[2]
     row_step = lin.shape[0] // (2 * stations)
     phase_rows(fringe, fringe_rate, stations, phases)
-    coarse[...] = coarse_columns(fringe_rate, stations)
-    tap_rows(filter_taps, taps)
+    tap_rows(filter_taps, fringe_rate, stations, pair, taps)
     blocks = (frames + P_SIZE - 1) * SUB + EARLY
     spread(volts, P_SIZE * SUB - EARLY, blocks, 0, stations, row_step, lin)
-    filter_frames(delays, taps, stations, frames, row_step, lin, filt)
+    filter_frames(delays, fringe_rate, taps, stations, frames, row_step, lin, filt)
     butterflies(phases, stations, frames, filt, zs)
 
 
 def second_kernel(
-    delays, volts, early, late, taps, table, phases, coarse, before, out,
-    lin, filt, zs, cosines, sines, turned, packed, sems
+    delays, fringe_rate, volts, early, late, taps, table, phases, before, out,
+    lin, filt, zs, turned
 ):
     stations, blocks = volts.shape[1], volts.shape[2] // LANES
     frames = zs.shape[2]
     width = 2 * (before.shape[2] + frames)
     row_step = lin.shape[0] // (2 * stations)
-    sign = jnp.where(lax.broadcasted_iota(jnp.int32, (1, width), 1) < width // 2, -1.0, 1.0)
-    for s in range(stations):
-        rows = slice(s * K, (s + 1) * K)
-        cosines[rows, :] = jnp.broadcast_to(coarse[:, s : s + 1], (K, width))
-        sines[rows, :] = coarse[:, stations + s : stations + s + 1] * sign
     spread(early, 0, EARLY, 0, stations, row_step, lin)
     spread(volts, 0, (2 * P_SIZE - 1) * SUB, EARLY, stations, row_step, lin)
-    filter_frames(delays, taps, stations, P_SIZE, row_step, lin, filt)
+    filter_frames(delays, fringe_rate, taps, stations, P_SIZE, row_step, lin, filt)
     butterflies(phases, stations, P_SIZE, filt, zs)
     own = P_SIZE * SUB + EARLY
     spread(volts, blocks - own, own, 0, stations, row_step, lin)
     spread(late, 0, LATE, own, stations, row_step, lin)
-    filter_frames(delays, taps, stations, P_SIZE, row_step, lin, filt)
+    filter_frames(delays, fringe_rate, taps, stations, P_SIZE, row_step, lin, filt)
     butterflies(phases, stations, P_SIZE, filt, zs, P_SIZE)
-
-    def sent(r, slot):
-        return pltpu.make_async_copy(packed.at[slot], out.at[:, r], sems.at[slot])
-
-    for r in range(RADIX):
-        slot = r % 2
-        weights = table[r * K : (r + 1) * K, :]
-        for s0 in range(0, stations, 2):
-            sides = []
-            for s in (s0, s0 + 1):
-                z = jnp.concatenate([before[r, s], zs[r, s]], axis=0)
-                sides += [z, jnp.concatenate([z[:, K:], -z[:, :K]], axis=1)]
-            both = lax.dot_general(
-                weights,
-                jnp.concatenate(sides, axis=0),
-                (((1,), (1,)), ((), ())),
-                preferred_element_type=F32,
-            )
-            for s in (s0, s0 + 1):
-                rows = slice(s * K, (s + 1) * K)
-                spec = both[:, (s - s0) * width : (s - s0 + 1) * width]
-                cross = pltpu.roll(spec, width // 2, 1)
-                rotated = spec * cosines[rows, :] + cross * sines[rows, :]
-                turned[pl.ds(s, K, stride=stations + 1), :] = rotated
-        if r >= 2:
-            sent(r - 2, slot).wait()
-        for k in range(K):
-            top = k * (stations + 1)
-            packed[slot, k] = turned[top : top + stations, :].astype(BF16)
-        sent(r, slot).start()
-    sent(RADIX - 2, 0).wait()
-    sent(RADIX - 1, 1).wait()
+    step = stations + 1
+    for s in range(stations):
+        rest = fringe_rate[s] & (RADIX - 1)
+        weights = table[pl.ds(pl.multiple_of(rest * K, K), K), :]
+        sides = []
+        for r in range(RADIX):
+            z = jnp.concatenate([before[s, r], zs[s, r]], axis=0)
+            sides += [z, jnp.concatenate([z[:, K:], -z[:, :K]], axis=1)]
+        spec = lax.dot_general(
+            weights,
+            jnp.concatenate(sides, axis=0),
+            (((1,), (1,)), ((), ())),
+            preferred_element_type=F32,
+        )
+        for r in range(RADIX):
+            part = spec[:, r * width : (r + 1) * width]
+            turned[pl.ds(r * (K * step) + s, K, stride=step), :] = part
+    for k in range(K):
+        for r in range(RADIX):
+            top = (r * K + k) * step
+            out[k, r] = turned[top : top + stations, :].astype(BF16)
 
 
 def rows_of(count):
@@ -256,18 +265,18 @@
     )(voltages)
     late = from_behind(late, "tm", -1)
     early = from_behind(early, "tm", 1)
-    step = ROW_PAD + EARLY + (ahead + P_SIZE - 1) * SUB + 1
-    before, phases, coarse, taps = pl.pallas_call(
+    step = ROW_PAD + EARLY + (ahead + P_SIZE - 1) * SUB + ROW_END
+    before, phases, taps = pl.pallas_call(
         first_kernel,
         out_shape=[
-            jax.ShapeDtypeStruct((RADIX, stations, ahead, 2 * K), BF16),
-            jax.ShapeDtypeStruct((stations * SUB, LANES), F32),
-            jax.ShapeDtypeStruct((K, LANES), F32),
-            jax.ShapeDtypeStruct((P_SIZE * SUB, LANES), F32),
+            jax.ShapeDtypeStruct((stations, RADIX, ahead, 2 * K), BF16),
+            jax.ShapeDtypeStruct((K // LANES * stations * SUB, LANES), F32),
+            jax.ShapeDtypeStruct((stations * P_SIZE * SUB, LANES), F32),
         ],
         in_specs=[smem, smem, smem, vmem, vmem],
-        out_specs=[vmem] * 4,
+        out_specs=[vmem] * 3,
         scratch_shapes=[
+            pltpu.VMEM(((2 * P_SIZE + 1) * SUB, LANES), F32),
             pltpu.VMEM((rows_of(2 * stations * step), LANES), F32),
             pltpu.VMEM((2 * stations * ahead * STEP, LANES), F32),
         ],
@@ -275,27 +284,23 @@
         cost_estimate=estimate,
         name="first",
     )(delays, fringe, fringe_rate, voltages, filter_taps)
-    step = ROW_PAD + EARLY + (2 * P_SIZE - 1) * SUB + 1
+    step = ROW_PAD + EARLY + (2 * P_SIZE - 1) * SUB + ROW_END
     return pl.pallas_call(
         second_kernel,
         out_shape=jax.ShapeDtypeStruct((K, RADIX, stations, 2 * frames), BF16),
-        in_specs=[smem] + [vmem] * 8,
-        out_specs=anywhere,
+        in_specs=[smem] * 2 + [vmem] * 7,
+        out_specs=vmem,
         scratch_shapes=[
             pltpu.VMEM((rows_of(2 * stations * step), LANES), F32),
             pltpu.VMEM((2 * stations * P_SIZE * STEP, LANES), F32),
-            pltpu.VMEM((RADIX, stations, rest, 2 * K), BF16),
-            pltpu.VMEM((stations * K, 2 * frames), F32),
-            pltpu.VMEM((stations * K, 2 * frames), F32),
-            pltpu.VMEM((K * (stations + 1), 2 * frames), F32),
-            pltpu.VMEM((2, K, stations, 2 * frames), BF16),
-            pltpu.SemaphoreType.DMA((2,)),
+            pltpu.VMEM((stations, RADIX, rest, 2 * K), BF16),
+            pltpu.VMEM((RADIX * K * (stations + 1), 2 * frames), F32),
         ],
-        compiler_params=pltpu.CompilerParams(vmem_limit_bytes=40 * 2**20),
+        compiler_params=pltpu.CompilerParams(vmem_limit_bytes=36 * 2**20),
         cost_estimate=estimate,
         name="second",
     )(
-        delays, voltages, early, late, taps, jnp.asarray(dft_table()), phases, coarse, before
+        delays, fringe_rate, voltages, early, late, taps, jnp.asarray(dft_table()), phases, before
     )
 
 

time: 109 us -> 106 us (0.972)
  Pallas kernels: 35.5 us -> 34 us
    pallas_call x1, Pallas kernels: 16.3 us -> 13.2 us  [front(): pl.pallas_call(second_kernel, out_shape=jax.ShapeDtypeStruct((K, RADIX, s...]
    pallas_call x1, Pallas kernels: 8.65 us -> 10.2 us  [front(): pl.pallas_call(first_kernel, out_shape=[jax.ShapeDtypeStruct((stations, R...]
  transfers between devices with their start and end apart: 2 -> 2, of which waited for: 1 -> 0; matrix products, arithmetic and copies ran while one was open for 0% -> 0% of each run, Pallas kernels for 8% -> 10%
where the time goes in v4:
time: 106 us
  blocking collectives  65 us (61%)
  Pallas kernels  34 us (32%)
  starting transfers between devices  5.68 us (5%)
    all_to_all x1, blocking collectives, local(): lax.all_to_all(outgoing, ('stn', 'tm'), split_axis=0, concat_axis=0, tile...  65 us
    pallas_call x1, Pallas kernels, front(): pl.pallas_call(second_kernel, out_shape=jax.ShapeDtypeStruct((K, RADIX, s...  13.2 us
    pallas_call x1, Pallas kernels, front(): pl.pallas_call(first_kernel, out_shape=[jax.ShapeDtypeStruct((stations, R...  10.2 us
    pallas_call x1, Pallas kernels, gram(): pl.pallas_call(body, grid=(channels,), out_shape=(shape, shape), in_specs...  8.25 us
    ppermute x2, starting transfers between devices, from_behind(): return lax.ppermute(block, axis, route)  5.68 us
    pallas_call x1, Pallas kernels, front(): pl.pallas_call(rims_kernel, out_shape=[jax.ShapeDtypeStruct((2, stations,...  2.36 us
  transfers between devices with their start and end apart: 2, of which 0 were waited for; matrix products, arithmetic and copies ran while one was open for 0% of the time, Pallas kernels for 10%

profile of v4, /device:TPU:7, one launch (start us, length us, event | category | flops | bytes accessed | tf_op | source)
XLA Modules:
  0.0 106.3 jit_solution(15785575381235270356)
XLA Ops:
  0.6 0.0 copy-start
  0.6 0.0 copy-start.4
  0.7 0.0 copy-start.3
  0.7 0.0 copy-start.2
  0.7 2.4 %rims.1 = (bf16[2,16,2048]{2,1,0:T(8,128)(2,1)}, bf16[2,16,15360]{2,1,0:T(8,128)(2,1)}) custom-call(bf16[2,16,65536]{2,1,0:T(8,128)(2,1)} %volts.5), custom_call_target="tpu_custom_call" | custom-call | tf_op jit(solution)/shard_map/rims/pallas_call | solution.py:254
  3.0 2.6 %collective-permute-start.1 = (bf16[2,16,15360]{2,1,0:T(8,128)(2,1)}, bf16[2,16,15360]{2,1,0:T(8,128)(2,1)S(1)}, u32[]{:S(2)}, u32[]{:S(2)}) collective-permute-start(bf16[2,16,15360]{2,1,0:T(8,128)(2,1)} %get-tuple-element.8), channel_id=1, source_target_pairs={{1,0},{2,1},{3,2},{5,4},{6,5},{7,6},{9,8},{10,9},{11,10},{13,12},{... | collective-permute-start | bytes 2949128 | tf_op jit(solution)/shard_map/ppermute | solution.py:27
  5.6 3.1 %collective-permute-start = (bf16[2,16,2048]{2,1,0:T(8,128)(2,1)}, bf16[2,16,2048]{2,1,0:T(8,128)(2,1)S(1)}, u32[]{:S(2)}, u32[]{:S(2)}) collective-permute-start(bf16[2,16,2048]{2,1,0:T(8,128)(2,1)} %get-tuple-element.7), channel_id=1, source_target_pairs={{0,1},{1,2},{2,3},{4,5},{5,6},{6,7},{8,9},{9,10},{10,11},{12,13},{... | collective-permute-start | bytes 393224 | tf_op jit(solution)/shard_map/ppermute | solution.py:27
  8.7 0.0 copy-done
  8.7 0.0 copy-done.4
  8.8 0.0 copy-done.3
  8.8 0.0 copy-done.2
  8.8 0.0 copy-start.1
  8.8 0.8 copy-done.1
  9.6 0.0 copy-start.5
  9.6 10.2 %first.1 = (bf16[16,4,32,512]{3,2,1,0:T(8,128)(2,1)S(1)}, f32[256,128]{1,0:T(8,128)S(1)}, f32[2048,128]{1,0:T(8,128)S(1)}) custom-call(s32[16]{0:T(128)S(1)} %copy-done.3, s32[16]{0:T(128)S(1)} %copy-done.2, s32[16]{0:T(128)S(1)} %copy-done.4, bf16[2,16,65536]{2,1,0:T(8,128)(2,1)S(1)} %copy-done, f32[16,1024]{1,0:T(8,128)S(1)} %copy-done.1), custom_call_target="tpu_custom_call" | custom-call | flops 10000000000 | bytes 8388608 | tf_op jit(solution)/shard_map/first/pallas_call | solution.py:269
  19.8 0.0 collective-permute-done.early
  19.8 0.0 collective-permute-done.1.late
  19.8 0.0 copy-done.5
  19.8 13.2 %second.1 = bf16[256,4,16,128]{3,2,1,0:T(8,128)(2,1)S(1)} custom-call(s32[16]{0:T(128)S(1)} %copy-done.3, s32[16]{0:T(128)S(1)} %copy-done.4, bf16[2,16,65536]{2,1,0:T(8,128)(2,1)S(1)} %copy-done, bf16[2,16,2048]{2,1,0:T(8,128)(2,1)S(1)} %collective-permute-done.early, bf16[2,16,15360]{2,1,0:T(8,128)(2,1)S(1)} %collective-permute-done.1.late, ...), custom_call_target="tpu_custom_call" | custom-call | flops 10000000000 | bytes 8388608 | tf_op jit(solution)/shard_map/second/pallas_call | solution.py:288
  33.1 65.0 %all_to_all.5.received = bf16[128,8,16,128]{3,2,1,0:T(8,128)(2,1)S(1)} all-to-all(bf16[128,8,16,128]{3,2,1,0:T(8,128)(2,1)S(1)} %bitcast.1), channel_id=1, replica_groups=mesh['stn'=32,'tm'=4] {'stn','tm'}, dimensions={0} | all-to-all | bytes 8388608 | tf_op jit(solution)/shard_map/all_to_all | solution.py:352
  98.1 8.2 %gram.1 = (f32[8,512,512]{2,1,0:T(8,128)}, f32[8,512,512]{2,1,0:T(8,128)}) custom-call(bf16[128,8,16,128]{3,2,1,0:T(8,128)(2,1)S(1)} %all_to_all.5.received), custom_call_target="tpu_custom_call" | custom-call | tf_op jit(solution)/shard_map/gram/pallas_call | solution.py:333
Async XLA Ops:
  0.6 8.1 %copy-start = (bf16[2,16,65536]{2,1,0:T(8,128)(2,1)S(1)}, bf16[2,16,65536]{2,1,0:T(8,128)(2,1)}, u32[]{:S(2)}) copy-start(bf16[2,16,65536]{2,1,0:T(8,128)(2,1)} %volts.5) | copy-start | bytes 12582916
  0.6 8.1 %copy-start.4 = (s32[16]{0:T(128)S(1)}, s32[16]{0:T(128)}, u32[]{:S(2)}) copy-start(s32[16]{0:T(128)} %fringe_rate.3) | copy-start | bytes 196
  0.7 8.1 %copy-start.3 = (s32[16]{0:T(128)S(1)}, s32[16]{0:T(128)}, u32[]{:S(2)}) copy-start(s32[16]{0:T(128)} %delays.3) | copy-start | bytes 196
  0.7 8.1 %copy-start.2 = (s32[16]{0:T(128)S(1)}, s32[16]{0:T(128)}, u32[]{:S(2)}) copy-start(s32[16]{0:T(128)} %fringe.1) | copy-start | bytes 196
  3.0 16.8 %collective-permute-start.1 = (bf16[2,16,15360]{2,1,0:T(8,128)(2,1)}, bf16[2,16,15360]{2,1,0:T(8,128)(2,1)S(1)}, u32[]{:S(2)}, u32[]{:S(2)}) collective-permute-start(bf16[2,16,15360]{2,1,0:T(8,128)(2,1)} %get-tuple-element.8), channel_id=1, source_target_pairs={{1,0},{2,1},{3,2},{5,4},{6,5},{7,6},{9,8},{10,9},{11,10},{13,12},{... | collective-permute-start | bytes 2949128 | tf_op jit(solution)/shard_map/ppermute | solution.py:27
  5.6 14.2 %collective-permute-start = (bf16[2,16,2048]{2,1,0:T(8,128)(2,1)}, bf16[2,16,2048]{2,1,0:T(8,128)(2,1)S(1)}, u32[]{:S(2)}, u32[]{:S(2)}) collective-permute-start(bf16[2,16,2048]{2,1,0:T(8,128)(2,1)} %get-tuple-element.7), channel_id=1, source_target_pairs={{0,1},{1,2},{2,3},{4,5},{5,6},{6,7},{8,9},{9,10},{10,11},{12,13},{... | collective-permute-start | bytes 393224 | tf_op jit(solution)/shard_map/ppermute | solution.py:27
  8.8 0.8 copy-start.1
  9.6 10.2 %copy-start.5 = (bf16[1024,512]{1,0:T(8,128)(2,1)S(1)}, bf16[1024,512]{1,0:T(8,128)(2,1)}, u32[]{:S(2)}) copy-start(bf16[1024,512]{1,0:T(8,128)(2,1)} %constant.2.clone.table) | copy-start | bytes 3145732

commit v5 on v4

--- a/solution.py
+++ b/solution.py
@@ -133,10 +133,10 @@
                 filt[pl.ds((row * frames + m) * STEP, SUB), :] = sums.pop(m)
         return carry
 
-    lax.fori_loop(0, 2 * stations, filter_row, 0, unroll=2)
-
-
-def butterflies(phases, stations, frames, filt, zs, top=0):
+    lax.fori_loop(0, 2 * stations, filter_row, 0, unroll=8)
+
+
+def butterflies(phases, stations, frames, filt, zs):
     def body(s, carry):
         def load(part, j):
             start = (part * stations + s) * (frames * STEP) + j
@@ -160,8 +160,8 @@
                 sine = phases[pl.ds((half * stations + s) * SUB + 2 * r + 1, 1), :]
                 zr = z[r][0] * cosine - z[r][1] * sine
                 zi = z[r][0] * sine + z[r][1] * cosine
-                zs[s, r, top : top + frames, pl.ds(half * LANES, LANES)] = zr.astype(BF16)
-                zs[s, r, top : top + frames, pl.ds(K + half * LANES, LANES)] = zi.astype(BF16)
+                zs[s, r, :, pl.ds(half * LANES, LANES)] = zr.astype(BF16)
+                zs[s, r, :, pl.ds(K + half * LANES, LANES)] = zi.astype(BF16)
         return carry
 
     lax.fori_loop(0, stations, body, 0)
@@ -185,36 +185,32 @@
 
 
 def first_kernel(
-    delays, fringe, fringe_rate, volts, filter_taps, zs, phases, taps, pair, lin, filt
+    delays, fringe, fringe_rate, volts, early, filter_taps, zs, phases, taps, pair, lin, filt
 ):
     stations = volts.shape[1]
     frames = zs.shape[2]
     row_step = lin.shape[0] // (2 * stations)
     phase_rows(fringe, fringe_rate, stations, phases)
     tap_rows(filter_taps, fringe_rate, stations, pair, taps)
-    blocks = (frames + P_SIZE - 1) * SUB + EARLY
-    spread(volts, P_SIZE * SUB - EARLY, blocks, 0, stations, row_step, lin)
+    spread(early, 0, EARLY, 0, stations, row_step, lin)
+    spread(volts, 0, (frames + P_SIZE - 1) * SUB, EARLY, stations, row_step, lin)
     filter_frames(delays, fringe_rate, taps, stations, frames, row_step, lin, filt)
     butterflies(phases, stations, frames, filt, zs)
 
 
 def second_kernel(
-    delays, fringe_rate, volts, early, late, taps, table, phases, before, out,
+    delays, fringe_rate, volts, late, taps, table, phases, before, out,
     lin, filt, zs, turned
 ):
     stations, blocks = volts.shape[1], volts.shape[2] // LANES
     frames = zs.shape[2]
     width = 2 * (before.shape[2] + frames)
     row_step = lin.shape[0] // (2 * stations)
-    spread(early, 0, EARLY, 0, stations, row_step, lin)
-    spread(volts, 0, (2 * P_SIZE - 1) * SUB, EARLY, stations, row_step, lin)
-    filter_frames(delays, fringe_rate, taps, stations, P_SIZE, row_step, lin, filt)
-    butterflies(phases, stations, P_SIZE, filt, zs)
     own = P_SIZE * SUB + EARLY
     spread(volts, blocks - own, own, 0, stations, row_step, lin)
     spread(late, 0, LATE, own, stations, row_step, lin)
     filter_frames(delays, fringe_rate, taps, stations, P_SIZE, row_step, lin, filt)
-    butterflies(phases, stations, P_SIZE, filt, zs, P_SIZE)
+    butterflies(phases, stations, P_SIZE, filt, zs)
     step = stations + 1
     for s in range(stations):
         rest = fringe_rate[s] & (RADIX - 1)
@@ -245,7 +241,7 @@
 def front(voltages, delays, fringe, fringe_rate, filter_taps):
     stations, samples = voltages.shape[1], voltages.shape[2]
     frames = samples // C
-    rest = 2 * P_SIZE
+    rest = P_SIZE
     ahead = frames - rest
     vmem = pl.BlockSpec(memory_space=pltpu.VMEM)
     smem = pl.BlockSpec(memory_space=pltpu.SMEM)
@@ -263,8 +259,8 @@
         compiler_params=pltpu.CompilerParams(vmem_limit_bytes=57 * 2**20),
         name="rims",
     )(voltages)
+    early = from_behind(early, "tm", 1)
     late = from_behind(late, "tm", -1)
-    early = from_behind(early, "tm", 1)
     step = ROW_PAD + EARLY + (ahead + P_SIZE - 1) * SUB + ROW_END
     before, phases, taps = pl.pallas_call(
         first_kernel,
@@ -273,7 +269,7 @@
             jax.ShapeDtypeStruct((K // LANES * stations * SUB, LANES), F32),
             jax.ShapeDtypeStruct((stations * P_SIZE * SUB, LANES), F32),
         ],
-        in_specs=[smem, smem, smem, vmem, vmem],
+        in_specs=[smem, smem, smem, vmem, vmem, vmem],
         out_specs=[vmem] * 3,
         scratch_shapes=[
             pltpu.VMEM(((2 * P_SIZE + 1) * SUB, LANES), F32),
@@ -283,12 +279,12 @@
         compiler_params=pltpu.CompilerParams(vmem_limit_bytes=28 * 2**20),
         cost_estimate=estimate,
         name="first",
-    )(delays, fringe, fringe_rate, voltages, filter_taps)
+    )(delays, fringe, fringe_rate, voltages, early, filter_taps)
     step = ROW_PAD + EARLY + (2 * P_SIZE - 1) * SUB + ROW_END
     return pl.pallas_call(
         second_kernel,
         out_shape=jax.ShapeDtypeStruct((K, RADIX, stations, 2 * frames), BF16),
-        in_specs=[smem] * 2 + [vmem] * 7,
+        in_specs=[smem] * 2 + [vmem] * 6,
         out_specs=vmem,
         scratch_shapes=[
             pltpu.VMEM((rows_of(2 * stations * step), LANES), F32),
@@ -300,14 +296,15 @@
         cost_estimate=estimate,
         name="second",
     )(
-        delays, fringe_rate, voltages, early, late, taps, jnp.asarray(dft_table()), phases, before
+        delays, fringe_rate, voltages, late, taps, jnp.asarray(dft_table()), phases, before
     )
 
 
 def gram_kernel(scale, groups, times, received, real, imag):
-    stations, width = received.shape[1], received.shape[2]
+    stations, width = received.shape[2], received.shape[3]
     half = width // 2
-    tiles = received[...].reshape(groups, times, stations, width)
+    channel = pl.program_id(0)
+    tiles = received[:, channel].reshape(groups, times, stations, width)
     direct, swapped = [], []
     for t in range(times):
         tile = tiles[:, t].reshape(groups * stations, width)
@@ -334,7 +331,7 @@
         body,
         grid=(channels,),
         out_shape=(shape, shape),
-        in_specs=[pl.BlockSpec((devices, None, stations, width), lambda c: (0, c, 0, 0))],
+        in_specs=[pl.BlockSpec(memory_space=pltpu.VMEM)],
         out_specs=(block, block),
         compiler_params=pltpu.CompilerParams(vmem_limit_bytes=48 * 1024 * 1024),
         name="gram",

time: 106 us -> 104 us (0.981)
  Pallas kernels: 34 us -> 30.1 us
    pallas_call x1, Pallas kernels: 13.2 us -> 7.35 us  [front(): pl.pallas_call(second_kernel, out_shape=jax.ShapeDtypeStruct((K, RADIX, s...]
    pallas_call x1, Pallas kernels: 10.2 us -> 12.5 us  [front(): pl.pallas_call(first_kernel, out_shape=[jax.ShapeDtypeStruct((stations, R...]
  transfers between devices with their start and end apart: 2 -> 2, of which waited for: 0 -> 1; matrix products, arithmetic and copies ran while one was open for 0% -> 0% of each run, Pallas kernels for 10% -> 12%
where the time goes in v5:
time: 104 us
  blocking collectives  66 us (63%)
  Pallas kernels  30.1 us (29%)
  starting transfers between devices  5.68 us (5%)
    all_to_all x1, blocking collectives, local(): lax.all_to_all(outgoing, ('stn', 'tm'), split_axis=0, concat_axis=0, tile...  66 us
    pallas_call x1, Pallas kernels, front(): pl.pallas_call(first_kernel, out_shape=[jax.ShapeDtypeStruct((stations, R...  12.5 us
    pallas_call x1, Pallas kernels, gram(): pl.pallas_call(body, grid=(channels,), out_shape=(shape, shape), in_specs...  7.88 us
    pallas_call x1, Pallas kernels, front(): pl.pallas_call(second_kernel, out_shape=jax.ShapeDtypeStruct((K, RADIX, s...  7.35 us
    ppermute x2, starting transfers between devices, from_behind(): return lax.ppermute(block, axis, route)  5.68 us
    pallas_call x1, Pallas kernels, front(): pl.pallas_call(rims_kernel, out_shape=[jax.ShapeDtypeStruct((2, stations,...  2.36 us
  transfers between devices with their start and end apart: 2, of which 1 were waited for; matrix products, arithmetic and copies ran while one was open for 0% of the time, Pallas kernels for 12%

profile of v5, /device:TPU:7, one launch (start us, length us, event | category | flops | bytes accessed | tf_op | source)
XLA Modules:
  0.0 103.7 jit_solution(4483543106093287679)
XLA Ops:
  0.6 0.0 copy-start
  0.6 0.0 copy-start.4
  0.7 0.0 copy-start.3
  0.7 0.0 copy-start.2
  0.7 2.4 %rims.1 = (bf16[2,16,2048]{2,1,0:T(8,128)(2,1)}, bf16[2,16,15360]{2,1,0:T(8,128)(2,1)}) custom-call(bf16[2,16,65536]{2,1,0:T(8,128)(2,1)} %volts.5), custom_call_target="tpu_custom_call" | custom-call | tf_op jit(solution)/shard_map/rims/pallas_call | solution.py:250
  3.0 3.8 %collective-permute-start.1 = (bf16[2,16,2048]{2,1,0:T(8,128)(2,1)}, bf16[2,16,2048]{2,1,0:T(8,128)(2,1)S(1)}, u32[]{:S(2)}, u32[]{:S(2)}) collective-permute-start(bf16[2,16,2048]{2,1,0:T(8,128)(2,1)} %get-tuple-element.8), channel_id=1, source_target_pairs={{0,1},{1,2},{2,3},{4,5},{5,6},{6,7},{8,9},{9,10},{10,11},{12,13},{... | collective-permute-start | bytes 393224 | tf_op jit(solution)/shard_map/ppermute | solution.py:27
  6.8 1.9 %collective-permute-start = (bf16[2,16,15360]{2,1,0:T(8,128)(2,1)}, bf16[2,16,15360]{2,1,0:T(8,128)(2,1)S(1)}, u32[]{:S(2)}, u32[]{:S(2)}) collective-permute-start(bf16[2,16,15360]{2,1,0:T(8,128)(2,1)} %get-tuple-element.7), channel_id=1, source_target_pairs={{1,0},{2,1},{3,2},{5,4},{6,5},{7,6},{9,8},{10,9},{11,10},{13,12},{... | collective-permute-start | bytes 2949128 | tf_op jit(solution)/shard_map/ppermute | solution.py:27
  8.7 0.3 collective-permute-done.1.early
  9.1 0.0 copy-done
  9.1 0.0 copy-done.4
  9.1 0.0 copy-done.3
  9.1 0.0 copy-done.2
  9.1 0.0 copy-start.1
  9.1 0.8 copy-done.1
  9.9 0.0 copy-start.5
  9.9 12.5 %first.1 = (bf16[16,4,48,512]{3,2,1,0:T(8,128)(2,1)S(1)}, f32[256,128]{1,0:T(8,128)S(1)}, f32[2048,128]{1,0:T(8,128)S(1)}) custom-call(s32[16]{0:T(128)S(1)} %copy-done.3, s32[16]{0:T(128)S(1)} %copy-done.2, s32[16]{0:T(128)S(1)} %copy-done.4, bf16[2,16,65536]{2,1,0:T(8,128)(2,1)S(1)} %copy-done, bf16[2,16,2048]{2,1,0:T(8,128)(2,1)S(1)} %collective-permute-done.1.early, ...), custom_call_target="tpu_custom_call" | custom-call | flops 10000000000 | bytes 8388608 | tf_op jit(solution)/shard_map/first/pallas_call | solution.py:265
  22.4 0.0 collective-permute-done.late
  22.5 0.0 copy-done.5
  22.5 7.4 %second.1 = bf16[256,4,16,128]{3,2,1,0:T(8,128)(2,1)S(1)} custom-call(s32[16]{0:T(128)S(1)} %copy-done.3, s32[16]{0:T(128)S(1)} %copy-done.4, bf16[2,16,65536]{2,1,0:T(8,128)(2,1)S(1)} %copy-done, bf16[2,16,15360]{2,1,0:T(8,128)(2,1)S(1)} %collective-permute-done.late, f32[2048,128]{1,0:T(8,128)S(1)} %get-tuple-element.9.taps, ...), custom_call_target="tpu_custom_call" | custom-call | flops 10000000000 | bytes 8388608 | tf_op jit(solution)/shard_map/second/pallas_call | solution.py:284
  29.8 66.0 %all_to_all.5.received = bf16[128,8,16,128]{3,2,1,0:T(8,128)(2,1)S(1)} all-to-all(bf16[128,8,16,128]{3,2,1,0:T(8,128)(2,1)S(1)} %bitcast.1), channel_id=1, replica_groups=mesh['stn'=32,'tm'=4] {'stn','tm'}, dimensions={0} | all-to-all | bytes 8388608 | tf_op jit(solution)/shard_map/all_to_all | solution.py:349
  95.8 7.9 %gram.1 = (f32[8,512,512]{2,1,0:T(8,128)}, f32[8,512,512]{2,1,0:T(8,128)}) custom-call(bf16[128,8,16,128]{3,2,1,0:T(8,128)(2,1)S(1)} %all_to_all.5.received), custom_call_target="tpu_custom_call" | custom-call | tf_op jit(solution)/shard_map/gram/pallas_call | solution.py:330
Async XLA Ops:
  0.6 8.4 %copy-start = (bf16[2,16,65536]{2,1,0:T(8,128)(2,1)S(1)}, bf16[2,16,65536]{2,1,0:T(8,128)(2,1)}, u32[]{:S(2)}) copy-start(bf16[2,16,65536]{2,1,0:T(8,128)(2,1)} %volts.5) | copy-start | bytes 12582916
  0.6 8.4 %copy-start.4 = (s32[16]{0:T(128)S(1)}, s32[16]{0:T(128)}, u32[]{:S(2)}) copy-start(s32[16]{0:T(128)} %fringe_rate.3) | copy-start | bytes 196
  0.7 8.4 %copy-start.3 = (s32[16]{0:T(128)S(1)}, s32[16]{0:T(128)}, u32[]{:S(2)}) copy-start(s32[16]{0:T(128)} %delays.3) | copy-start | bytes 196
  0.7 8.4 %copy-start.2 = (s32[16]{0:T(128)S(1)}, s32[16]{0:T(128)}, u32[]{:S(2)}) copy-start(s32[16]{0:T(128)} %fringe.1) | copy-start | bytes 196
  3.0 6.0 %collective-permute-start.1 = (bf16[2,16,2048]{2,1,0:T(8,128)(2,1)}, bf16[2,16,2048]{2,1,0:T(8,128)(2,1)S(1)}, u32[]{:S(2)}, u32[]{:S(2)}) collective-permute-start(bf16[2,16,2048]{2,1,0:T(8,128)(2,1)} %get-tuple-element.8), channel_id=1, source_target_pairs={{0,1},{1,2},{2,3},{4,5},{5,6},{6,7},{8,9},{9,10},{10,11},{12,13},{... | collective-permute-start | bytes 393224 | tf_op jit(solution)/shard_map/ppermute | solution.py:27
  6.8 15.6 %collective-permute-start = (bf16[2,16,15360]{2,1,0:T(8,128)(2,1)}, bf16[2,16,15360]{2,1,0:T(8,128)(2,1)S(1)}, u32[]{:S(2)}, u32[]{:S(2)}) collective-permute-start(bf16[2,16,15360]{2,1,0:T(8,128)(2,1)} %get-tuple-element.7), channel_id=1, source_target_pairs={{1,0},{2,1},{3,2},{5,4},{6,5},{7,6},{9,8},{10,9},{11,10},{13,12},{... | collective-permute-start | bytes 2949128 | tf_op jit(solution)/shard_map/ppermute | solution.py:27
  9.1 0.8 copy-start.1
  9.9 12.6 %copy-start.5 = (bf16[1024,512]{1,0:T(8,128)(2,1)S(1)}, bf16[1024,512]{1,0:T(8,128)(2,1)}, u32[]{:S(2)}) copy-start(bf16[1024,512]{1,0:T(8,128)(2,1)} %constant.2.clone.table) | copy-start | bytes 3145732

commit v6 on v5

--- a/solution.py
+++ b/solution.py
@@ -58,12 +58,12 @@
 
 
 def tap_rows(filter_taps, fringe_rate, stations, pair, taps):
-    for p in range(P_SIZE):
+    for p in range(0, P_SIZE, SUB):
         for j in range(SUB):
-            piece = filter_taps[p : p + 1, j * LANES : (j + 1) * LANES]
+            piece = filter_taps[p : p + SUB, j * LANES : (j + 1) * LANES]
             for copy in range(2):
-                row = SUB + (2 * p + copy) * SUB + j
-                pair[row : row + 1, :] = piece
+                start = SUB + (2 * p + copy) * SUB + j
+                pair[pl.ds(start, SUB, stride=2 * SUB), :] = piece
     lane = lax.broadcasted_iota(jnp.int32, (SUB, LANES), 1)
 
     def body(s, carry):
@@ -78,7 +78,7 @@
             taps[pl.ds(top, SUB), :] = pltpu.roll(jnp.where(keep, here, before), shift, 1)
         return carry
 
-    lax.fori_loop(0, stations, body, 0)
+    lax.fori_loop(0, stations, body, 0, unroll=4)
 
 
 def spread(source, first, count, offset, stations, row_step, lin):
@@ -256,7 +256,7 @@
         in_specs=[anywhere],
         out_specs=[vmem, vmem],
         scratch_shapes=[pltpu.SemaphoreType.DMA((2,))],
-        compiler_params=pltpu.CompilerParams(vmem_limit_bytes=57 * 2**20),
+        compiler_params=pltpu.CompilerParams(vmem_limit_bytes=52 * 2**20),
         name="rims",
     )(voltages)
     early = from_behind(early, "tm", 1)

time: 104 us -> 102 us (0.981)
  Pallas kernels: 30.1 us -> 28.3 us
  transfers between devices with their start and end apart: 2 -> 2, of which waited for: 1 -> 1; matrix products, arithmetic and copies ran while one was open for 0% -> 0% of each run, Pallas kernels for 12% -> 11%
where the time goes in v6:
time: 102 us
  blocking collectives  65.2 us (64%)
  Pallas kernels  28.3 us (28%)
  starting transfers between devices  5.82 us (6%)
    all_to_all x1, blocking collectives, local(): lax.all_to_all(outgoing, ('stn', 'tm'), split_axis=0, concat_axis=0, tile...  65.2 us
    pallas_call x1, Pallas kernels, front(): pl.pallas_call(first_kernel, out_shape=[jax.ShapeDtypeStruct((stations, R...  11.7 us
    pallas_call x1, Pallas kernels, gram(): pl.pallas_call(body, grid=(channels,), out_shape=(shape, shape), in_specs...  7.87 us
    pallas_call x1, Pallas kernels, front(): pl.pallas_call(second_kernel, out_shape=jax.ShapeDtypeStruct((K, RADIX, s...  7.35 us
    ppermute x2, starting transfers between devices, from_behind(): return lax.ppermute(block, axis, route)  5.82 us
  transfers between devices with their start and end apart: 2, of which 1 were waited for; matrix products, arithmetic and copies ran while one was open for 0% of the time, Pallas kernels for 11%

profile of v6, /device:TPU:7, one launch (start us, length us, event | category | flops | bytes accessed | tf_op | source)
XLA Modules:
  0.0 101.8 jit_solution(12120625101777614432)
XLA Ops:
  0.6 0.0 copy-start
  0.6 0.0 copy-start.4
  0.7 0.0 copy-start.3
  0.7 0.0 copy-start.2
  0.7 1.4 %rims.1 = (bf16[2,16,2048]{2,1,0:T(8,128)(2,1)S(1)}, bf16[2,16,15360]{2,1,0:T(8,128)(2,1)S(1)}) custom-call(bf16[2,16,65536]{2,1,0:T(8,128)(2,1)} %volts.5), custom_call_target="tpu_custom_call" | custom-call | tf_op jit(solution)/shard_map/rims/pallas_call | solution.py:250
  2.0 3.9 %collective-permute-start.1 = (bf16[2,16,2048]{2,1,0:T(8,128)(2,1)S(1)}, bf16[2,16,2048]{2,1,0:T(8,128)(2,1)S(1)}, u32[]{:S(2)}, u32[]{:S(2)}) collective-permute-start(bf16[2,16,2048]{2,1,0:T(8,128)(2,1)S(1)} %get-tuple-element.8), channel_id=1, source_target_pairs={{0,1},{1,2},{2,3},{4,5},{5,6},{6,7},{8,9},{9,10},{10,11},{12,13},{... | collective-permute-start | bytes 393224 | tf_op jit(solution)/shard_map/ppermute | solution.py:27
  6.0 1.9 %collective-permute-start = (bf16[2,16,15360]{2,1,0:T(8,128)(2,1)S(1)}, bf16[2,16,15360]{2,1,0:T(8,128)(2,1)S(1)}, u32[]{:S(2)}, u32[]{:S(2)}) collective-permute-start(bf16[2,16,15360]{2,1,0:T(8,128)(2,1)S(1)} %get-tuple-element.7), channel_id=1, source_target_pairs={{1,0},{2,1},{3,2},{5,4},{6,5},{7,6},{9,8},{10,9},{11,10},{13,12},{... | collective-permute-start | bytes 2949128 | tf_op jit(solution)/shard_map/ppermute | solution.py:27
  7.9 0.0 collective-permute-done.1.early
  7.9 0.0 copy-done
  7.9 0.0 copy-done.4
  7.9 0.0 copy-done.3
  7.9 0.0 copy-done.2
  7.9 0.0 copy-start.1
  7.9 0.8 copy-done.1
  8.8 0.0 copy-start.5
  8.8 11.7 %first.1 = (bf16[16,4,48,512]{3,2,1,0:T(8,128)(2,1)S(1)}, f32[256,128]{1,0:T(8,128)S(1)}, f32[2048,128]{1,0:T(8,128)S(1)}) custom-call(s32[16]{0:T(128)S(1)} %copy-done.3, s32[16]{0:T(128)S(1)} %copy-done.2, s32[16]{0:T(128)S(1)} %copy-done.4, bf16[2,16,65536]{2,1,0:T(8,128)(2,1)S(1)} %copy-done, bf16[2,16,2048]{2,1,0:T(8,128)(2,1)S(1)} %collective-permute-done.1.early, ...), custom_call_target="tpu_custom_call" | custom-call | flops 10000000000 | bytes 8388608 | tf_op jit(solution)/shard_map/first/pallas_call | solution.py:265
  20.5 0.9 collective-permute-done.late
  21.4 0.0 copy-done.5
  21.4 7.3 %second.1 = bf16[256,4,16,128]{3,2,1,0:T(8,128)(2,1)S(1)} custom-call(s32[16]{0:T(128)S(1)} %copy-done.3, s32[16]{0:T(128)S(1)} %copy-done.4, bf16[2,16,65536]{2,1,0:T(8,128)(2,1)S(1)} %copy-done, bf16[2,16,15360]{2,1,0:T(8,128)(2,1)S(1)} %collective-permute-done.late, f32[2048,128]{1,0:T(8,128)S(1)} %get-tuple-element.9.taps, ...), custom_call_target="tpu_custom_call" | custom-call | flops 10000000000 | bytes 8388608 | tf_op jit(solution)/shard_map/second/pallas_call | solution.py:284
  28.7 65.2 %all_to_all.5.received = bf16[128,8,16,128]{3,2,1,0:T(8,128)(2,1)S(1)} all-to-all(bf16[128,8,16,128]{3,2,1,0:T(8,128)(2,1)S(1)} %bitcast.1), channel_id=1, replica_groups=mesh['stn'=32,'tm'=4] {'stn','tm'}, dimensions={0} | all-to-all | bytes 8388608 | tf_op jit(solution)/shard_map/all_to_all | solution.py:349
  93.9 7.9 %gram.1 = (f32[8,512,512]{2,1,0:T(8,128)}, f32[8,512,512]{2,1,0:T(8,128)}) custom-call(bf16[128,8,16,128]{3,2,1,0:T(8,128)(2,1)S(1)} %all_to_all.5.received), custom_call_target="tpu_custom_call" | custom-call | tf_op jit(solution)/shard_map/gram/pallas_call | solution.py:330
Async XLA Ops:
  0.6 7.3 %copy-start = (bf16[2,16,65536]{2,1,0:T(8,128)(2,1)S(1)}, bf16[2,16,65536]{2,1,0:T(8,128)(2,1)}, u32[]{:S(2)}) copy-start(bf16[2,16,65536]{2,1,0:T(8,128)(2,1)} %volts.5) | copy-start | bytes 12582916
  0.6 7.3 %copy-start.4 = (s32[16]{0:T(128)S(1)}, s32[16]{0:T(128)}, u32[]{:S(2)}) copy-start(s32[16]{0:T(128)} %fringe_rate.3) | copy-start | bytes 196
  0.7 7.3 %copy-start.3 = (s32[16]{0:T(128)S(1)}, s32[16]{0:T(128)}, u32[]{:S(2)}) copy-start(s32[16]{0:T(128)} %delays.3) | copy-start | bytes 196
  0.7 7.3 %copy-start.2 = (s32[16]{0:T(128)S(1)}, s32[16]{0:T(128)}, u32[]{:S(2)}) copy-start(s32[16]{0:T(128)} %fringe.1) | copy-start | bytes 196
  2.0 5.8 %collective-permute-start.1 = (bf16[2,16,2048]{2,1,0:T(8,128)(2,1)S(1)}, bf16[2,16,2048]{2,1,0:T(8,128)(2,1)S(1)}, u32[]{:S(2)}, u32[]{:S(2)}) collective-permute-start(bf16[2,16,2048]{2,1,0:T(8,128)(2,1)S(1)} %get-tuple-element.8), channel_id=1, source_target_pairs={{0,1},{1,2},{2,3},{4,5},{5,6},{6,7},{8,9},{9,10},{10,11},{12,13},{... | collective-permute-start | bytes 393224 | tf_op jit(solution)/shard_map/ppermute | solution.py:27
  6.0 15.4 %collective-permute-start = (bf16[2,16,15360]{2,1,0:T(8,128)(2,1)S(1)}, bf16[2,16,15360]{2,1,0:T(8,128)(2,1)S(1)}, u32[]{:S(2)}, u32[]{:S(2)}) collective-permute-start(bf16[2,16,15360]{2,1,0:T(8,128)(2,1)S(1)} %get-tuple-element.7), channel_id=1, source_target_pairs={{1,0},{2,1},{3,2},{5,4},{6,5},{7,6},{9,8},{10,9},{11,10},{13,12},{... | collective-permute-start | bytes 2949128 | tf_op jit(solution)/shard_map/ppermute | solution.py:27
  7.9 0.8 copy-start.1
  8.8 12.6 %copy-start.5 = (bf16[1024,512]{1,0:T(8,128)(2,1)S(1)}, bf16[1024,512]{1,0:T(8,128)(2,1)}, u32[]{:S(2)}) copy-start(bf16[1024,512]{1,0:T(8,128)(2,1)} %constant.2.clone.table) | copy-start | bytes 3145732

commit v7 on v6

--- a/solution.py
+++ b/solution.py
@@ -95,7 +95,8 @@
                     lin[pl.ds(start, SUB, stride=row_step), :] = tile[top : top + SUB]
         return carry
 
-    lax.fori_loop(0, count // unroll, body, 0)
+    steps = count // unroll
+    lax.fori_loop(0, steps, body, 0, unroll=next(u for u in (5, 3, 2, 1) if steps % u == 0))
 
 
 def filter_frames(delays, fringe_rate, taps, stations, frames, row_step, lin, filt):
@@ -133,7 +134,7 @@
                 filt[pl.ds((row * frames + m) * STEP, SUB), :] = sums.pop(m)
         return carry
 
-    lax.fori_loop(0, 2 * stations, filter_row, 0, unroll=8)
+    lax.fori_loop(0, 2 * stations, filter_row, 0, unroll=8 if frames > P_SIZE else 16)
 
 
 def butterflies(phases, stations, frames, filt, zs):
@@ -164,7 +165,7 @@
                 zs[s, r, :, pl.ds(K + half * LANES, LANES)] = zi.astype(BF16)
         return carry
 
-    lax.fori_loop(0, stations, body, 0)
+    lax.fori_loop(0, stations, body, 0, unroll=4)
 
 
 def rims_kernel(volts, early, late, sems):

time: 102 us -> 101 us (level)
  no operation moved by 1% of the time
where the time goes in v7:
time: 101 us
  blocking collectives  64.9 us (64%)
  Pallas kernels  27.7 us (27%)
  starting transfers between devices  5.82 us (6%)
  waiting for transfers between devices  1.17 us (1%)
    all_to_all x1, blocking collectives, local(): lax.all_to_all(outgoing, ('stn', 'tm'), split_axis=0, concat_axis=0, tile...  64.9 us
    pallas_call x1, Pallas kernels, front(): pl.pallas_call(first_kernel, out_shape=[jax.ShapeDtypeStruct((stations, R...  11.4 us
    pallas_call x1, Pallas kernels, gram(): pl.pallas_call(body, grid=(channels,), out_shape=(shape, shape), in_specs...  7.87 us
    pallas_call x1, Pallas kernels, front(): pl.pallas_call(second_kernel, out_shape=jax.ShapeDtypeStruct((K, RADIX, s...  6.99 us
    ppermute x2, starting transfers between devices, from_behind(): return lax.ppermute(block, axis, route)  5.82 us
  transfers between devices with their start and end apart: 2, of which 1 were waited for; matrix products, arithmetic and copies ran while one was open for 0% of the time, Pallas kernels for 11%

profile of v7, /device:TPU:7, one launch (start us, length us, event | category | flops | bytes accessed | tf_op | source)
XLA Modules:
  0.0 101.2 jit_solution(10086713698606523395)
XLA Ops:
  0.6 0.0 copy-start
  0.6 0.0 copy-start.4
  0.7 0.0 copy-start.3
  0.7 0.0 copy-start.2
  0.7 1.4 %rims.1 = (bf16[2,16,2048]{2,1,0:T(8,128)(2,1)S(1)}, bf16[2,16,15360]{2,1,0:T(8,128)(2,1)S(1)}) custom-call(bf16[2,16,65536]{2,1,0:T(8,128)(2,1)} %volts.5), custom_call_target="tpu_custom_call" | custom-call | tf_op jit(solution)/shard_map/rims/pallas_call | solution.py:251
  2.0 3.9 %collective-permute-start.1 = (bf16[2,16,2048]{2,1,0:T(8,128)(2,1)S(1)}, bf16[2,16,2048]{2,1,0:T(8,128)(2,1)S(1)}, u32[]{:S(2)}, u32[]{:S(2)}) collective-permute-start(bf16[2,16,2048]{2,1,0:T(8,128)(2,1)S(1)} %get-tuple-element.8), channel_id=1, source_target_pairs={{0,1},{1,2},{2,3},{4,5},{5,6},{6,7},{8,9},{9,10},{10,11},{12,13},{... | collective-permute-start | bytes 393224 | tf_op jit(solution)/shard_map/ppermute | solution.py:27
  6.0 1.9 %collective-permute-start = (bf16[2,16,15360]{2,1,0:T(8,128)(2,1)S(1)}, bf16[2,16,15360]{2,1,0:T(8,128)(2,1)S(1)}, u32[]{:S(2)}, u32[]{:S(2)}) collective-permute-start(bf16[2,16,15360]{2,1,0:T(8,128)(2,1)S(1)} %get-tuple-element.7), channel_id=1, source_target_pairs={{1,0},{2,1},{3,2},{5,4},{6,5},{7,6},{9,8},{10,9},{11,10},{13,12},{... | collective-permute-start | bytes 2949128 | tf_op jit(solution)/shard_map/ppermute | solution.py:27
  7.9 0.0 collective-permute-done.1.early
  7.9 0.0 copy-done
  7.9 0.0 copy-done.4
  7.9 0.0 copy-done.3
  7.9 0.0 copy-done.2
  7.9 0.0 copy-start.1
  7.9 0.8 copy-done.1
  8.8 0.0 copy-start.5
  8.8 11.4 %first.1 = (bf16[16,4,48,512]{3,2,1,0:T(8,128)(2,1)S(1)}, f32[256,128]{1,0:T(8,128)S(1)}, f32[2048,128]{1,0:T(8,128)S(1)}) custom-call(s32[16]{0:T(128)S(1)} %copy-done.3, s32[16]{0:T(128)S(1)} %copy-done.2, s32[16]{0:T(128)S(1)} %copy-done.4, bf16[2,16,65536]{2,1,0:T(8,128)(2,1)S(1)} %copy-done, bf16[2,16,2048]{2,1,0:T(8,128)(2,1)S(1)} %collective-permute-done.1.early, ...), custom_call_target="tpu_custom_call" | custom-call | flops 10000000000 | bytes 8388608 | tf_op jit(solution)/shard_map/first/pallas_call | solution.py:266
  20.2 1.2 %collective-permute-done.late = bf16[2,16,15360]{2,1,0:T(8,128)(2,1)S(1)} collective-permute-done((bf16[2,16,15360]{2,1,0:T(8,128)(2,1)S(1)}, bf16[2,16,15360]{2,1,0:T(8,128)(2,1)S(1)}, u32[]{:S(2)}, u32[]{:S(2)}) %collective-permute-start) | collective-permute-done | bytes 983072 | tf_op jit(solution)/shard_map/ppermute | solution.py:27
  21.4 0.0 copy-done.5
  21.4 7.0 %second.1 = bf16[256,4,16,128]{3,2,1,0:T(8,128)(2,1)S(1)} custom-call(s32[16]{0:T(128)S(1)} %copy-done.3, s32[16]{0:T(128)S(1)} %copy-done.4, bf16[2,16,65536]{2,1,0:T(8,128)(2,1)S(1)} %copy-done, bf16[2,16,15360]{2,1,0:T(8,128)(2,1)S(1)} %collective-permute-done.late, f32[2048,128]{1,0:T(8,128)S(1)} %get-tuple-element.9.taps, ...), custom_call_target="tpu_custom_call" | custom-call | flops 10000000000 | bytes 8388608 | tf_op jit(solution)/shard_map/second/pallas_call | solution.py:285
  28.4 64.9 %all_to_all.5.received = bf16[128,8,16,128]{3,2,1,0:T(8,128)(2,1)S(1)} all-to-all(bf16[128,8,16,128]{3,2,1,0:T(8,128)(2,1)S(1)} %bitcast.1), channel_id=1, replica_groups=mesh['stn'=32,'tm'=4] {'stn','tm'}, dimensions={0} | all-to-all | bytes 8388608 | tf_op jit(solution)/shard_map/all_to_all | solution.py:350
  93.3 7.9 %gram.1 = (f32[8,512,512]{2,1,0:T(8,128)}, f32[8,512,512]{2,1,0:T(8,128)}) custom-call(bf16[128,8,16,128]{3,2,1,0:T(8,128)(2,1)S(1)} %all_to_all.5.received), custom_call_target="tpu_custom_call" | custom-call | tf_op jit(solution)/shard_map/gram/pallas_call | solution.py:331
Async XLA Ops:
  0.6 7.3 %copy-start = (bf16[2,16,65536]{2,1,0:T(8,128)(2,1)S(1)}, bf16[2,16,65536]{2,1,0:T(8,128)(2,1)}, u32[]{:S(2)}) copy-start(bf16[2,16,65536]{2,1,0:T(8,128)(2,1)} %volts.5) | copy-start | bytes 12582916
  0.6 7.3 %copy-start.4 = (s32[16]{0:T(128)S(1)}, s32[16]{0:T(128)}, u32[]{:S(2)}) copy-start(s32[16]{0:T(128)} %fringe_rate.3) | copy-start | bytes 196
  0.7 7.3 %copy-start.3 = (s32[16]{0:T(128)S(1)}, s32[16]{0:T(128)}, u32[]{:S(2)}) copy-start(s32[16]{0:T(128)} %delays.3) | copy-start | bytes 196
  0.7 7.3 %copy-start.2 = (s32[16]{0:T(128)S(1)}, s32[16]{0:T(128)}, u32[]{:S(2)}) copy-start(s32[16]{0:T(128)} %fringe.1) | copy-start | bytes 196
  2.0 5.8 %collective-permute-start.1 = (bf16[2,16,2048]{2,1,0:T(8,128)(2,1)S(1)}, bf16[2,16,2048]{2,1,0:T(8,128)(2,1)S(1)}, u32[]{:S(2)}, u32[]{:S(2)}) collective-permute-start(bf16[2,16,2048]{2,1,0:T(8,128)(2,1)S(1)} %get-tuple-element.8), channel_id=1, source_target_pairs={{0,1},{1,2},{2,3},{4,5},{5,6},{6,7},{8,9},{9,10},{10,11},{12,13},{... | collective-permute-start | bytes 393224 | tf_op jit(solution)/shard_map/ppermute | solution.py:27
  6.0 15.4 %collective-permute-start = (bf16[2,16,15360]{2,1,0:T(8,128)(2,1)S(1)}, bf16[2,16,15360]{2,1,0:T(8,128)(2,1)S(1)}, u32[]{:S(2)}, u32[]{:S(2)}) collective-permute-start(bf16[2,16,15360]{2,1,0:T(8,128)(2,1)S(1)} %get-tuple-element.7), channel_id=1, source_target_pairs={{1,0},{2,1},{3,2},{5,4},{6,5},{7,6},{9,8},{10,9},{11,10},{13,12},{... | collective-permute-start | bytes 2949128 | tf_op jit(solution)/shard_map/ppermute | solution.py:27
  7.9 0.8 copy-start.1
  8.8 12.6 %copy-start.5 = (bf16[1024,512]{1,0:T(8,128)(2,1)S(1)}, bf16[1024,512]{1,0:T(8,128)(2,1)}, u32[]{:S(2)}) copy-start(bf16[1024,512]{1,0:T(8,128)(2,1)} %constant.2.clone.table) | copy-start | bytes 3145732

commit v8 on v7

--- a/solution.py
+++ b/solution.py
@@ -131,7 +131,8 @@
                     sums[m] = sums[m] + term if m in sums else term
             m = k - (P_SIZE - 1)
             if m >= 0:
-                filt[pl.ds((row * frames + m) * STEP, SUB), :] = sums.pop(m)
+                weighted = sums.pop(m).astype(BF16).astype(F32)
+                filt[pl.ds((row * frames + m) * STEP, SUB), :] = weighted
         return carry
 
     lax.fori_loop(0, 2 * stations, filter_row, 0, unroll=8 if frames > P_SIZE else 16)

time: 101 us -> 102 us (level)
  transfers between devices with their start and end apart: 2 -> 2, of which waited for: 1 -> 1; matrix products, arithmetic and copies ran while one was open for 0% -> 0% of each run, Pallas kernels for 11% -> 12%
where the time goes in v8:
time: 102 us
  blocking collectives  65.3 us (64%)
  Pallas kernels  28.1 us (28%)
  starting transfers between devices  5.82 us (6%)
    all_to_all x1, blocking collectives, local(): lax.all_to_all(outgoing, ('stn', 'tm'), split_axis=0, concat_axis=0, tile...  65.3 us
    pallas_call x1, Pallas kernels, front(): pl.pallas_call(first_kernel, out_shape=[jax.ShapeDtypeStruct((stations, R...  11.8 us
    pallas_call x1, Pallas kernels, gram(): pl.pallas_call(body, grid=(channels,), out_shape=(shape, shape), in_specs...  7.87 us
    pallas_call x1, Pallas kernels, front(): pl.pallas_call(second_kernel, out_shape=jax.ShapeDtypeStruct((K, RADIX, s...  7.07 us
    ppermute x2, starting transfers between devices, from_behind(): return lax.ppermute(block, axis, route)  5.82 us
  transfers between devices with their start and end apart: 2, of which 1 were waited for; matrix products, arithmetic and copies ran while one was open for 0% of the time, Pallas kernels for 12%

profile of v8, /device:TPU:7, one launch (start us, length us, event | category | flops | bytes accessed | tf_op | source)
XLA Modules:
  0.0 101.6 jit_solution(10175879152163881627)
XLA Ops:
  0.6 0.0 copy-start
  0.6 0.0 copy-start.4
  0.7 0.0 copy-start.3
  0.7 0.0 copy-start.2
  0.7 1.4 %rims.1 = (bf16[2,16,2048]{2,1,0:T(8,128)(2,1)S(1)}, bf16[2,16,15360]{2,1,0:T(8,128)(2,1)S(1)}) custom-call(bf16[2,16,65536]{2,1,0:T(8,128)(2,1)} %volts.5), custom_call_target="tpu_custom_call" | custom-call | tf_op jit(solution)/shard_map/rims/pallas_call | solution.py:252
  2.0 3.9 %collective-permute-start.1 = (bf16[2,16,2048]{2,1,0:T(8,128)(2,1)S(1)}, bf16[2,16,2048]{2,1,0:T(8,128)(2,1)S(1)}, u32[]{:S(2)}, u32[]{:S(2)}) collective-permute-start(bf16[2,16,2048]{2,1,0:T(8,128)(2,1)S(1)} %get-tuple-element.8), channel_id=1, source_target_pairs={{0,1},{1,2},{2,3},{4,5},{5,6},{6,7},{8,9},{9,10},{10,11},{12,13},{... | collective-permute-start | bytes 393224 | tf_op jit(solution)/shard_map/ppermute | solution.py:27
  6.0 1.9 %collective-permute-start = (bf16[2,16,15360]{2,1,0:T(8,128)(2,1)S(1)}, bf16[2,16,15360]{2,1,0:T(8,128)(2,1)S(1)}, u32[]{:S(2)}, u32[]{:S(2)}) collective-permute-start(bf16[2,16,15360]{2,1,0:T(8,128)(2,1)S(1)} %get-tuple-element.7), channel_id=1, source_target_pairs={{1,0},{2,1},{3,2},{5,4},{6,5},{7,6},{9,8},{10,9},{11,10},{13,12},{... | collective-permute-start | bytes 2949128 | tf_op jit(solution)/shard_map/ppermute | solution.py:27
  7.9 0.0 collective-permute-done.1.early
  7.9 0.0 copy-done
  7.9 0.0 copy-done.4
  7.9 0.0 copy-done.3
  7.9 0.0 copy-done.2
  7.9 0.0 copy-start.1
  7.9 0.8 copy-done.1
  8.8 0.0 copy-start.5
  8.8 11.8 %first.1 = (bf16[16,4,48,512]{3,2,1,0:T(8,128)(2,1)S(1)}, f32[256,128]{1,0:T(8,128)S(1)}, f32[2048,128]{1,0:T(8,128)S(1)}) custom-call(s32[16]{0:T(128)S(1)} %copy-done.3, s32[16]{0:T(128)S(1)} %copy-done.2, s32[16]{0:T(128)S(1)} %copy-done.4, bf16[2,16,65536]{2,1,0:T(8,128)(2,1)S(1)} %copy-done, bf16[2,16,2048]{2,1,0:T(8,128)(2,1)S(1)} %collective-permute-done.1.early, ...), custom_call_target="tpu_custom_call" | custom-call | flops 10000000000 | bytes 8388608 | tf_op jit(solution)/shard_map/first/pallas_call | solution.py:267
  20.5 0.8 collective-permute-done.late
  21.4 0.0 copy-done.5
  21.4 7.1 %second.1 = bf16[256,4,16,128]{3,2,1,0:T(8,128)(2,1)S(1)} custom-call(s32[16]{0:T(128)S(1)} %copy-done.3, s32[16]{0:T(128)S(1)} %copy-done.4, bf16[2,16,65536]{2,1,0:T(8,128)(2,1)S(1)} %copy-done, bf16[2,16,15360]{2,1,0:T(8,128)(2,1)S(1)} %collective-permute-done.late, f32[2048,128]{1,0:T(8,128)S(1)} %get-tuple-element.9.taps, ...), custom_call_target="tpu_custom_call" | custom-call | flops 10000000000 | bytes 8388608 | tf_op jit(solution)/shard_map/second/pallas_call | solution.py:286
  28.5 65.3 %all_to_all.5.received = bf16[128,8,16,128]{3,2,1,0:T(8,128)(2,1)S(1)} all-to-all(bf16[128,8,16,128]{3,2,1,0:T(8,128)(2,1)S(1)} %bitcast.1), channel_id=1, replica_groups=mesh['stn'=32,'tm'=4] {'stn','tm'}, dimensions={0} | all-to-all | bytes 8388608 | tf_op jit(solution)/shard_map/all_to_all | solution.py:351
  93.7 7.9 %gram.1 = (f32[8,512,512]{2,1,0:T(8,128)}, f32[8,512,512]{2,1,0:T(8,128)}) custom-call(bf16[128,8,16,128]{3,2,1,0:T(8,128)(2,1)S(1)} %all_to_all.5.received), custom_call_target="tpu_custom_call" | custom-call | tf_op jit(solution)/shard_map/gram/pallas_call | solution.py:332
Async XLA Ops:
  0.6 7.3 %copy-start = (bf16[2,16,65536]{2,1,0:T(8,128)(2,1)S(1)}, bf16[2,16,65536]{2,1,0:T(8,128)(2,1)}, u32[]{:S(2)}) copy-start(bf16[2,16,65536]{2,1,0:T(8,128)(2,1)} %volts.5) | copy-start | bytes 12582916
  0.6 7.3 %copy-start.4 = (s32[16]{0:T(128)S(1)}, s32[16]{0:T(128)}, u32[]{:S(2)}) copy-start(s32[16]{0:T(128)} %fringe_rate.3) | copy-start | bytes 196
  0.7 7.3 %copy-start.3 = (s32[16]{0:T(128)S(1)}, s32[16]{0:T(128)}, u32[]{:S(2)}) copy-start(s32[16]{0:T(128)} %delays.3) | copy-start | bytes 196
  0.7 7.3 %copy-start.2 = (s32[16]{0:T(128)S(1)}, s32[16]{0:T(128)}, u32[]{:S(2)}) copy-start(s32[16]{0:T(128)} %fringe.1) | copy-start | bytes 196
  2.0 5.8 %collective-permute-start.1 = (bf16[2,16,2048]{2,1,0:T(8,128)(2,1)S(1)}, bf16[2,16,2048]{2,1,0:T(8,128)(2,1)S(1)}, u32[]{:S(2)}, u32[]{:S(2)}) collective-permute-start(bf16[2,16,2048]{2,1,0:T(8,128)(2,1)S(1)} %get-tuple-element.8), channel_id=1, source_target_pairs={{0,1},{1,2},{2,3},{4,5},{5,6},{6,7},{8,9},{9,10},{10,11},{12,13},{... | collective-permute-start | bytes 393224 | tf_op jit(solution)/shard_map/ppermute | solution.py:27
  6.0 15.4 %collective-permute-start = (bf16[2,16,15360]{2,1,0:T(8,128)(2,1)S(1)}, bf16[2,16,15360]{2,1,0:T(8,128)(2,1)S(1)}, u32[]{:S(2)}, u32[]{:S(2)}) collective-permute-start(bf16[2,16,15360]{2,1,0:T(8,128)(2,1)S(1)} %get-tuple-element.7), channel_id=1, source_target_pairs={{1,0},{2,1},{3,2},{5,4},{6,5},{7,6},{9,8},{10,9},{11,10},{13,12},{... | collective-permute-start | bytes 2949128 | tf_op jit(solution)/shard_map/ppermute | solution.py:27
  7.9 0.8 copy-start.1
  8.8 12.6 %copy-start.5 = (bf16[1024,512]{1,0:T(8,128)(2,1)S(1)}, bf16[1024,512]{1,0:T(8,128)(2,1)}, u32[]{:S(2)}) copy-start(bf16[1024,512]{1,0:T(8,128)(2,1)} %constant.2.clone.table) | copy-start | bytes 3145732

commit v9 on v7

--- a/solution.py
+++ b/solution.py
@@ -134,7 +134,7 @@
                 filt[pl.ds((row * frames + m) * STEP, SUB), :] = sums.pop(m)
         return carry
 
-    lax.fori_loop(0, 2 * stations, filter_row, 0, unroll=8 if frames > P_SIZE else 16)
+    lax.fori_loop(0, 2 * stations, filter_row, 0, unroll=16)
 
 
 def butterflies(phases, stations, frames, filt, zs):

time: 101 us -> 101 us (level)
  no operation moved by 1% of the time
where the time goes in v9:
time: 101 us
  blocking collectives  64.8 us (64%)
  Pallas kernels  27.5 us (27%)
  starting transfers between devices  5.82 us (6%)
  waiting for transfers between devices  1.31 us (1%)
    all_to_all x1, blocking collectives, local(): lax.all_to_all(outgoing, ('stn', 'tm'), split_axis=0, concat_axis=0, tile...  64.8 us
    pallas_call x1, Pallas kernels, front(): pl.pallas_call(first_kernel, out_shape=[jax.ShapeDtypeStruct((stations, R...  11.3 us
    pallas_call x1, Pallas kernels, gram(): pl.pallas_call(body, grid=(channels,), out_shape=(shape, shape), in_specs...  7.87 us
    pallas_call x1, Pallas kernels, front(): pl.pallas_call(second_kernel, out_shape=jax.ShapeDtypeStruct((K, RADIX, s...  6.99 us
    ppermute x2, starting transfers between devices, from_behind(): return lax.ppermute(block, axis, route)  5.82 us
  transfers between devices with their start and end apart: 2, of which 1 were waited for; matrix products, arithmetic and copies ran while one was open for 0% of the time, Pallas kernels for 11%

profile of v9, /device:TPU:7, one launch (start us, length us, event | category | flops | bytes accessed | tf_op | source)
XLA Modules:
  0.0 101.1 jit_solution(12415384225937845048)
XLA Ops:
  0.6 0.0 copy-start
  0.6 0.0 copy-start.4
  0.7 0.0 copy-start.3
  0.7 0.0 copy-start.2
  0.7 1.4 %rims.1 = (bf16[2,16,2048]{2,1,0:T(8,128)(2,1)S(1)}, bf16[2,16,15360]{2,1,0:T(8,128)(2,1)S(1)}) custom-call(bf16[2,16,65536]{2,1,0:T(8,128)(2,1)} %volts.5), custom_call_target="tpu_custom_call" | custom-call | tf_op jit(solution)/shard_map/rims/pallas_call | solution.py:251
  2.0 3.9 %collective-permute-start.1 = (bf16[2,16,2048]{2,1,0:T(8,128)(2,1)S(1)}, bf16[2,16,2048]{2,1,0:T(8,128)(2,1)S(1)}, u32[]{:S(2)}, u32[]{:S(2)}) collective-permute-start(bf16[2,16,2048]{2,1,0:T(8,128)(2,1)S(1)} %get-tuple-element.8), channel_id=1, source_target_pairs={{0,1},{1,2},{2,3},{4,5},{5,6},{6,7},{8,9},{9,10},{10,11},{12,13},{... | collective-permute-start | bytes 393224 | tf_op jit(solution)/shard_map/ppermute | solution.py:27
  6.0 1.9 %collective-permute-start = (bf16[2,16,15360]{2,1,0:T(8,128)(2,1)S(1)}, bf16[2,16,15360]{2,1,0:T(8,128)(2,1)S(1)}, u32[]{:S(2)}, u32[]{:S(2)}) collective-permute-start(bf16[2,16,15360]{2,1,0:T(8,128)(2,1)S(1)} %get-tuple-element.7), channel_id=1, source_target_pairs={{1,0},{2,1},{3,2},{5,4},{6,5},{7,6},{9,8},{10,9},{11,10},{13,12},{... | collective-permute-start | bytes 2949128 | tf_op jit(solution)/shard_map/ppermute | solution.py:27
  7.9 0.0 collective-permute-done.1.early
  7.9 0.0 copy-done
  7.9 0.0 copy-done.4
  7.9 0.0 copy-done.3
  7.9 0.0 copy-done.2
  7.9 0.0 copy-start.1
  7.9 0.8 copy-done.1
  8.8 0.0 copy-start.5
  8.8 11.3 %first.1 = (bf16[16,4,48,512]{3,2,1,0:T(8,128)(2,1)S(1)}, f32[256,128]{1,0:T(8,128)S(1)}, f32[2048,128]{1,0:T(8,128)S(1)}) custom-call(s32[16]{0:T(128)S(1)} %copy-done.3, s32[16]{0:T(128)S(1)} %copy-done.2, s32[16]{0:T(128)S(1)} %copy-done.4, bf16[2,16,65536]{2,1,0:T(8,128)(2,1)S(1)} %copy-done, bf16[2,16,2048]{2,1,0:T(8,128)(2,1)S(1)} %collective-permute-done.1.early, ...), custom_call_target="tpu_custom_call" | custom-call | flops 10000000000 | bytes 8388608 | tf_op jit(solution)/shard_map/first/pallas_call | solution.py:266
  20.1 1.3 %collective-permute-done.late = bf16[2,16,15360]{2,1,0:T(8,128)(2,1)S(1)} collective-permute-done((bf16[2,16,15360]{2,1,0:T(8,128)(2,1)S(1)}, bf16[2,16,15360]{2,1,0:T(8,128)(2,1)S(1)}, u32[]{:S(2)}, u32[]{:S(2)}) %collective-permute-start) | collective-permute-done | bytes 983072 | tf_op jit(solution)/shard_map/ppermute | solution.py:27
  21.4 0.0 copy-done.5
  21.4 7.0 %second.1 = bf16[256,4,16,128]{3,2,1,0:T(8,128)(2,1)S(1)} custom-call(s32[16]{0:T(128)S(1)} %copy-done.3, s32[16]{0:T(128)S(1)} %copy-done.4, bf16[2,16,65536]{2,1,0:T(8,128)(2,1)S(1)} %copy-done, bf16[2,16,15360]{2,1,0:T(8,128)(2,1)S(1)} %collective-permute-done.late, f32[2048,128]{1,0:T(8,128)S(1)} %get-tuple-element.9.taps, ...), custom_call_target="tpu_custom_call" | custom-call | flops 10000000000 | bytes 8388608 | tf_op jit(solution)/shard_map/second/pallas_call | solution.py:285
  28.4 64.8 %all_to_all.5.received = bf16[128,8,16,128]{3,2,1,0:T(8,128)(2,1)S(1)} all-to-all(bf16[128,8,16,128]{3,2,1,0:T(8,128)(2,1)S(1)} %bitcast.1), channel_id=1, replica_groups=mesh['stn'=32,'tm'=4] {'stn','tm'}, dimensions={0} | all-to-all | bytes 8388608 | tf_op jit(solution)/shard_map/all_to_all | solution.py:350
  93.2 7.9 %gram.1 = (f32[8,512,512]{2,1,0:T(8,128)}, f32[8,512,512]{2,1,0:T(8,128)}) custom-call(bf16[128,8,16,128]{3,2,1,0:T(8,128)(2,1)S(1)} %all_to_all.5.received), custom_call_target="tpu_custom_call" | custom-call | tf_op jit(solution)/shard_map/gram/pallas_call | solution.py:331
Async XLA Ops:
  0.6 7.3 %copy-start = (bf16[2,16,65536]{2,1,0:T(8,128)(2,1)S(1)}, bf16[2,16,65536]{2,1,0:T(8,128)(2,1)}, u32[]{:S(2)}) copy-start(bf16[2,16,65536]{2,1,0:T(8,128)(2,1)} %volts.5) | copy-start | bytes 12582916
  0.6 7.3 %copy-start.4 = (s32[16]{0:T(128)S(1)}, s32[16]{0:T(128)}, u32[]{:S(2)}) copy-start(s32[16]{0:T(128)} %fringe_rate.3) | copy-start | bytes 196
  0.7 7.3 %copy-start.3 = (s32[16]{0:T(128)S(1)}, s32[16]{0:T(128)}, u32[]{:S(2)}) copy-start(s32[16]{0:T(128)} %delays.3) | copy-start | bytes 196
  0.7 7.3 %copy-start.2 = (s32[16]{0:T(128)S(1)}, s32[16]{0:T(128)}, u32[]{:S(2)}) copy-start(s32[16]{0:T(128)} %fringe.1) | copy-start | bytes 196
  2.0 5.8 %collective-permute-start.1 = (bf16[2,16,2048]{2,1,0:T(8,128)(2,1)S(1)}, bf16[2,16,2048]{2,1,0:T(8,128)(2,1)S(1)}, u32[]{:S(2)}, u32[]{:S(2)}) collective-permute-start(bf16[2,16,2048]{2,1,0:T(8,128)(2,1)S(1)} %get-tuple-element.8), channel_id=1, source_target_pairs={{0,1},{1,2},{2,3},{4,5},{5,6},{6,7},{8,9},{9,10},{10,11},{12,13},{... | collective-permute-start | bytes 393224 | tf_op jit(solution)/shard_map/ppermute | solution.py:27
  6.0 15.4 %collective-permute-start = (bf16[2,16,15360]{2,1,0:T(8,128)(2,1)S(1)}, bf16[2,16,15360]{2,1,0:T(8,128)(2,1)S(1)}, u32[]{:S(2)}, u32[]{:S(2)}) collective-permute-start(bf16[2,16,15360]{2,1,0:T(8,128)(2,1)S(1)} %get-tuple-element.7), channel_id=1, source_target_pairs={{1,0},{2,1},{3,2},{5,4},{6,5},{7,6},{9,8},{10,9},{11,10},{13,12},{... | collective-permute-start | bytes 2949128 | tf_op jit(solution)/shard_map/ppermute | solution.py:27
  7.9 0.8 copy-start.1
  8.8 12.6 %copy-start.5 = (bf16[1024,512]{1,0:T(8,128)(2,1)S(1)}, bf16[1024,512]{1,0:T(8,128)(2,1)}, u32[]{:S(2)}) copy-start(bf16[1024,512]{1,0:T(8,128)(2,1)} %constant.2.clone.table) | copy-start | bytes 3145732
